TPU v7x, 32 devices: a whole 2x2x4 slice. The times are simulated.
32 devices in a mesh: section: 2 (over core), dp: 4 (over y, x), seq: 4 (over z).
Axes of the slice: x: 2, y: 2, z: 4, core: 2. Of those that a mesh axis runs over, the one named last changes fastest.
Arguments:
- section_ends: bfloat16 [2, 2, 4, 1024, 512], P('section', None, 'dp', 'seq'), may hold values from -6 to 6
- live: int32 [2, 4], P(None, 'dp'), may hold values from 0 to 1, as said below
- norm_gains: bfloat16 [2, 2, 512], P('section', None, 'dp'), may hold values from 0.5 to 1.5
- offsets: bfloat16 [2, 6, 512], P('section', None, 'dp'), may hold values from -2.5 to 2.5
- expand_bias: bfloat16 [2, 2048], P('section', 'dp'), may hold values from -2.5 to 2.5
- query_key_value: bfloat16 [2, 512, 1536], P('section', 'dp'), may hold values from -0.25 to 0.25
- attention_out: bfloat16 [2, 512, 512], P('section', 'dp'), may hold values from -2 to 2
- expand_weight: bfloat16 [2, 512, 2048], P('section', 'dp'), may hold values from -0.25 to 0.25
- contract_weight: bfloat16 [2, 2048, 512], P('section', 'dp'), may hold values from -0.125 to 0.125
Outputs:
- section_edges: float32 [2, 2, 4, 1024, 512], P('section', None, 'dp', 'seq')
- grad_norm_gains: float32 [2, 2, 512], P('section', None, 'dp')
- grad_offsets: float32 [2, 6, 512], P('section', None, 'dp')
- grad_expand_bias: float32 [2, 2048], P('section', 'dp')
- grad_query_key_value: float32 [2, 512, 1536], P('section', 'dp')
- grad_attention_out: float32 [2, 512, 512], P('section', 'dp')
- grad_expand: float32 [2, 512, 2048], P('section', 'dp')
- grad_contract: float32 [2, 2048, 512], P('section', 'dp')
Inputs may be any that keep to these rules, and one draw needn't show every extreme that they name: `live`: 0 marks an empty slot of a micro-batch; in every draw some slot is 0 and some is 1.
All inputs are finite; a program needn't handle non-finite values.
Results may differ from a plain program's by a relative error of at most 0.018.
Values may be sent and summed in bfloat16 or wider, within the bound.
A program may use at most 128 MiB of HBM per device.

v0:
```python
import jax
import jax.numpy as jnp
from jax import lax
from jax.sharding import PartitionSpec as P

HD = 64


EPSILON = 1e-05


def from_behind(block, axis, distance):
    devices = range(lax.axis_size(axis))
    route = [(i - distance, i) for i in devices if i - distance in devices]
    return lax.ppermute(block, axis, route)


def layer_norm(values, gain, shift):
    row_mean = jnp.mean(values, axis=-1, keepdims=True)
    centred = values - row_mean
    variance = jnp.mean(centred * centred, axis=-1, keepdims=True)
    inverse = lax.rsqrt(variance + EPSILON)
    normal = centred * inverse
    return (normal * gain + shift, normal, inverse)


def norm_back(grad_norm, normal, inverse, gain):
    grad_gain = jnp.sum(grad_norm * normal, axis=0)
    grad_shift = jnp.sum(grad_norm, axis=0)
    scaled = grad_norm * gain
    centre_part = jnp.mean(scaled, axis=-1, keepdims=True)
    along_part = normal * jnp.mean(scaled * normal, axis=-1, keepdims=True)
    return (inverse * (scaled - centre_part - along_part), grad_gain, grad_shift)


def matmul(left, right):
    return jnp.dot(left, right, preferred_element_type=jnp.float32)


def dot_first(left, right):
    return lax.dot_general(
        left, right, (((0,), (0,)), ((), ())), preferred_element_type=jnp.float32
    )


def dot_last(left, right):
    return lax.dot_general(
        left, right, (((1,), (1,)), ((), ())), preferred_element_type=jnp.float32
    )


def gelu_tanh(values):
    return jax.nn.gelu(values, approximate=True)


def attend_forward(packed, head_dim):
    length = packed.shape[0]
    local_heads = packed.shape[2] // head_dim
    unpacked = packed.reshape(length, 3, local_heads, head_dim)
    queries = unpacked[:, 0]
    keys_all = unpacked[:, 1]
    values_all = unpacked[:, 2]
    block_rows = min(512, length)
    score_scale = head_dim ** (-0.5)
    key_place = jnp.arange(length)

    def one_block(start):
        query_rows = lax.dynamic_slice_in_dim(queries, start, block_rows, 0)
        scores = (
            jnp.einsum("qhd,khd->hqk", query_rows, keys_all, preferred_element_type=jnp.float32)
            * score_scale
        )
        query_place = start + jnp.arange(block_rows)
        causal = (key_place[None, :] <= query_place[:, None])[None]
        scores = jnp.where(causal, scores, -1e30)
        row_top = jnp.max(scores, axis=-1, keepdims=True)
        exp_scores = jnp.exp(scores - row_top)
        row_total = jnp.sum(exp_scores, axis=-1, keepdims=True)
        probabilities = (exp_scores / row_total).astype(jnp.bfloat16)
        result = jnp.einsum(
            "hqk,khd->qhd", probabilities, values_all, preferred_element_type=jnp.float32
        )
        return (result.astype(jnp.bfloat16), (row_top + jnp.log(row_total))[..., 0])

    block_starts = jnp.arange(length // block_rows) * block_rows
    results, log_totals = lax.map(one_block, block_starts)
    return (results.reshape(length, local_heads * head_dim), log_totals)


def attend_backward(packed, grad_heads, log_totals, head_dim):
    length = packed.shape[0]
    local_heads = packed.shape[2] // head_dim
    unpacked = packed.reshape(length, 3, local_heads, head_dim)
    queries = unpacked[:, 0]
    keys_all = unpacked[:, 1]
    values_all = unpacked[:, 2]
    grad_rows_all = grad_heads.reshape(length, local_heads, head_dim)
    block_rows = min(512, length)
    score_scale = head_dim ** (-0.5)
    key_place = jnp.arange(length)

    def one_block(carry, block_input):
        grad_keys, grad_values = carry
        start, block_lse = block_input
        query_rows = lax.dynamic_slice_in_dim(queries, start, block_rows, 0)
        grad_rows = lax.dynamic_slice_in_dim(grad_rows_all, start, block_rows, 0)
        scores = (
            jnp.einsum("qhd,khd->hqk", query_rows, keys_all, preferred_element_type=jnp.float32)
            * score_scale
        )
        query_place = start + jnp.arange(block_rows)
        causal = (key_place[None, :] <= query_place[:, None])[None]
        scores = jnp.where(causal, scores, -1e30)
        probabilities = jnp.exp(scores - block_lse[..., None])
        grad_probs = jnp.einsum(
            "qhd,khd->hqk", grad_rows, values_all, preferred_element_type=jnp.float32
        )
        grad_values = grad_values + jnp.einsum(
            "hqk,qhd->khd",
            probabilities.astype(jnp.bfloat16),
            grad_rows,
            preferred_element_type=jnp.float32,
        )
        inner = jnp.sum(probabilities * grad_probs, axis=-1, keepdims=True)
        grad_scores = (probabilities * (grad_probs - inner)).astype(jnp.bfloat16)
        grad_query = (
            jnp.einsum("hqk,khd->qhd", grad_scores, keys_all, preferred_element_type=jnp.float32)
            * score_scale
        )
        grad_keys = (
            grad_keys
            + jnp.einsum(
                "hqk,qhd->khd", grad_scores, query_rows, preferred_element_type=jnp.float32
            )
            * score_scale
        )
        return ((grad_keys, grad_values), grad_query)

    empty = jnp.zeros((length, local_heads, head_dim), jnp.float32)
    block_starts = jnp.arange(length // block_rows) * block_rows
    (grad_keys, grad_values), grad_queries = lax.scan(
        one_block, (empty, empty), (block_starts, log_totals)
    )
    grad_queries = grad_queries.reshape(length, local_heads, head_dim)
    stacked = jnp.stack([grad_queries, grad_keys, grad_values], axis=1).astype(jnp.bfloat16)
    return stacked.reshape(length, 3, local_heads * head_dim)


def section_forward(tokens_in, weights):
    gain_rows, shift_rows, bias_row, qkv_matrix, out_matrix, up_matrix, down_matrix = weights
    gain_float = gain_rows.astype(jnp.float32)
    shift_float = shift_rows.astype(jnp.float32)
    row_count = tokens_in.shape[0]
    model_width = out_matrix.shape[0]
    normed = layer_norm(tokens_in, gain_float[0], shift_float[0])[0]
    qkv_bias = jnp.concatenate([shift_float[1], jnp.zeros_like(shift_float[1]), shift_float[2]])
    qkv_tokens = (matmul(normed.astype(jnp.bfloat16), qkv_matrix) + qkv_bias).astype(jnp.bfloat16)
    qkv_heads = lax.all_to_all(
        qkv_tokens.reshape(row_count, 3, model_width),
        "seq",
        split_axis=2,
        concat_axis=0,
        tiled=True,
    )
    attended_heads, log_totals = attend_forward(qkv_heads, HD)
    attended = lax.all_to_all(attended_heads, "seq", split_axis=0, concat_axis=1, tiled=True)
    hidden = tokens_in + matmul(attended, out_matrix) + shift_float[3]
    normed_two = layer_norm(hidden, gain_float[1], shift_float[4])[0]
    upward = matmul(normed_two.astype(jnp.bfloat16), up_matrix) + bias_row.astype(jnp.float32)
    activated = gelu_tanh(upward).astype(jnp.bfloat16)
    result = hidden + matmul(activated, down_matrix) + shift_float[5]
    return (result, (qkv_heads, log_totals, attended, hidden, upward))


def section_backward(grad_out, saved, weights):
    gain_rows, shift_rows, bias_row, qkv_matrix, out_matrix, up_matrix, down_matrix = weights
    gain_float = gain_rows.astype(jnp.float32)
    shift_float = shift_rows.astype(jnp.float32)
    tokens_low, qkv_heads, log_totals, attended, hidden, upward = saved
    tokens_in = tokens_low.astype(jnp.float32)
    row_count = tokens_in.shape[0]
    model_width = out_matrix.shape[0]
    grad_branch = grad_out.astype(jnp.bfloat16)
    activated = gelu_tanh(upward).astype(jnp.bfloat16)
    grad_down = dot_first(activated, grad_branch)
    grad_down_bias = jnp.sum(grad_branch.astype(jnp.float32), axis=0)
    grad_act = dot_last(grad_branch, down_matrix)
    unused, gelu_pull = jax.vjp(gelu_tanh, upward)
    grad_upward = gelu_pull(grad_act)[0].astype(jnp.bfloat16)
    grad_up_bias = jnp.sum(grad_upward.astype(jnp.float32), axis=0)
    normed_two, normal_two, inverse_two = layer_norm(hidden, gain_float[1], shift_float[4])
    grad_up = dot_first(normed_two.astype(jnp.bfloat16), grad_upward)
    grad_normed_two = dot_last(grad_upward, up_matrix)
    grad_from_norm, grad_gain_two, grad_shift_two = norm_back(
        grad_normed_two, normal_two, inverse_two, gain_float[1]
    )
    grad_hidden = grad_out + grad_from_norm
    grad_residual = grad_hidden.astype(jnp.bfloat16)
    grad_out_bias = jnp.sum(grad_residual.astype(jnp.float32), axis=0)
    grad_out_matrix = dot_first(attended, grad_residual)
    grad_attended = dot_last(grad_residual, out_matrix).astype(jnp.bfloat16)
    grad_heads = lax.all_to_all(grad_attended, "seq", split_axis=1, concat_axis=0, tiled=True)
    grad_packed_heads = attend_backward(qkv_heads, grad_heads, log_totals, HD)
    grad_packed = lax.all_to_all(
        grad_packed_heads, "seq", split_axis=0, concat_axis=2, tiled=True
    ).reshape(row_count, 3 * model_width)
    grad_packed_float = grad_packed.astype(jnp.float32)
    grad_query_bias = jnp.sum(grad_packed_float[:, :model_width], axis=0)
    grad_value_bias = jnp.sum(grad_packed_float[:, 2 * model_width :], axis=0)
    normed, normal, inverse = layer_norm(tokens_in, gain_float[0], shift_float[0])
    grad_qkv_matrix = dot_first(normed.astype(jnp.bfloat16), grad_packed)
    grad_normed = dot_last(grad_packed, qkv_matrix)
    grad_from_first, grad_gain_one, grad_shift_one = norm_back(
        grad_normed, normal, inverse, gain_float[0]
    )
    grad_tokens = grad_hidden + grad_from_first
    grad_gains = jnp.stack([grad_gain_one, grad_gain_two])
    grad_shifts = jnp.stack(
        [
            grad_shift_one,
            grad_query_bias,
            grad_value_bias,
            grad_out_bias,
            grad_shift_two,
            grad_down_bias,
        ]
    )
    return (
        grad_tokens,
        (
            grad_gains,
            grad_shifts,
            grad_up_bias,
            grad_qkv_matrix,
            grad_out_matrix,
            grad_up,
            grad_down,
        ),
    )


def store(buffer_rows, value, place, is_valid):
    previous = lax.dynamic_index_in_dim(buffer_rows, place, 0, keepdims=False)
    chosen = jnp.where(is_valid, value, previous)
    return lax.dynamic_update_index_in_dim(buffer_rows, chosen, place, 0)


def shards(
    section_ends,
    live,
    norm_gains,
    offsets,
    expand_bias,
    query_key_value,
    attention_out,
    expand_weight,
    contract_weight,
):
    section_index = lax.axis_index("section")
    micro_count = section_ends.shape[1]
    local_ends = section_ends[0, :, 0]
    row_count = local_ends.shape[1]
    model_width = local_ends.shape[2]
    live_float = live[:, 0].astype(jnp.float32)
    weights = (
        lax.all_gather(norm_gains[0], "dp", axis=1, tiled=True),
        lax.all_gather(offsets[0], "dp", axis=1, tiled=True),
        lax.all_gather(expand_bias[0], "dp", axis=0, tiled=True),
        lax.all_gather(query_key_value[0], "dp", axis=0, tiled=True),
        lax.all_gather(attention_out[0], "dp", axis=0, tiled=True),
        lax.all_gather(expand_weight[0], "dp", axis=0, tiled=True),
        lax.all_gather(contract_weight[0], "dp", axis=0, tiled=True),
    )
    incoming = jnp.zeros((row_count, model_width), jnp.bfloat16)
    buffers = None
    outputs_mb = jnp.zeros((micro_count, row_count, model_width), jnp.float32)
    for step_number in range(micro_count + 1):
        index_mb = step_number - section_index
        is_valid = (index_mb >= 0) & (index_mb < micro_count)
        safe_index = jnp.clip(index_mb, 0, micro_count - 1)
        own_input = lax.dynamic_index_in_dim(local_ends, safe_index, 0, keepdims=False)
        tokens_low = jnp.where(section_index == 0, own_input, incoming)
        result, saved = section_forward(tokens_low.astype(jnp.float32), weights)
        record = (tokens_low,) + saved
        if buffers is None:
            buffers = tuple((jnp.zeros((micro_count,) + a.shape, a.dtype) for a in record))
        buffers = tuple((store(a, b, safe_index, is_valid) for a, b in zip(buffers, record)))
        outputs_mb = store(outputs_mb, result, safe_index, is_valid)
        if step_number < micro_count:
            incoming = from_behind(result.astype(jnp.bfloat16), "section", 1)
    weights_back = (
        lax.all_gather(norm_gains[0], "dp", axis=1, tiled=True),
        lax.all_gather(offsets[0], "dp", axis=1, tiled=True),
        lax.all_gather(expand_bias[0], "dp", axis=0, tiled=True),
        lax.all_gather(query_key_value[0], "dp", axis=0, tiled=True),
        lax.all_gather(attention_out[0], "dp", axis=0, tiled=True),
        lax.all_gather(expand_weight[0], "dp", axis=0, tiled=True),
        lax.all_gather(contract_weight[0], "dp", axis=0, tiled=True),
    )
    grad_sums = tuple((jnp.zeros(a.shape, jnp.float32) for a in weights_back))
    edge_grads = jnp.zeros((micro_count, row_count, model_width), jnp.float32)
    arriving = jnp.zeros((row_count, model_width), jnp.bfloat16)
    for step_number in range(micro_count + 1):
        index_mb = step_number - 1 + section_index
        is_valid = (index_mb >= 0) & (index_mb < micro_count)
        safe_index = jnp.clip(index_mb, 0, micro_count - 1)
        own_cotangent = lax.dynamic_index_in_dim(local_ends, safe_index, 0, keepdims=False).astype(
            jnp.float32
        )
        own_cotangent = own_cotangent * lax.dynamic_index_in_dim(
            live_float, safe_index, 0, keepdims=False
        )
        grad_out = jnp.where(section_index == 1, own_cotangent, arriving.astype(jnp.float32))
        saved = tuple((lax.dynamic_index_in_dim(a, safe_index, 0, keepdims=False) for a in buffers))
        grad_tokens, grads = section_backward(grad_out, saved, weights_back)
        grad_sums = tuple((a + jnp.where(is_valid, b, 0.0) for a, b in zip(grad_sums, grads)))
        edge_grads = store(edge_grads, grad_tokens, safe_index, is_valid)
        if step_number < micro_count:
            arriving = from_behind(grad_tokens.astype(jnp.bfloat16), "section", -1)
    sum_gains, sum_shifts, sum_bias, sum_qkv, sum_out, sum_up, sum_down = grad_sums
    total_gains, total_shifts, total_bias, total_qkv, total_out, total_up, total_down = (
        lax.psum(sum_gains.astype(jnp.bfloat16), "seq").astype(jnp.float32),
        lax.psum(sum_shifts.astype(jnp.bfloat16), "seq").astype(jnp.float32),
        lax.psum(sum_bias.astype(jnp.bfloat16), "seq").astype(jnp.float32),
        lax.psum(sum_qkv.astype(jnp.bfloat16), "seq").astype(jnp.float32),
        lax.psum(sum_out.astype(jnp.bfloat16), "seq").astype(jnp.float32),
        lax.psum(sum_up.astype(jnp.bfloat16), "seq").astype(jnp.float32),
        lax.psum(sum_down.astype(jnp.bfloat16), "seq").astype(jnp.float32),
    )
    final = (
        lax.psum_scatter(
            total_gains.astype(jnp.bfloat16), "dp", scatter_dimension=1, tiled=True
        ).astype(jnp.float32),
        lax.psum_scatter(
            total_shifts.astype(jnp.bfloat16), "dp", scatter_dimension=1, tiled=True
        ).astype(jnp.float32),
        lax.psum_scatter(
            total_bias.astype(jnp.bfloat16), "dp", scatter_dimension=0, tiled=True
        ).astype(jnp.float32),
        lax.psum_scatter(
            total_qkv.astype(jnp.bfloat16), "dp", scatter_dimension=0, tiled=True
        ).astype(jnp.float32),
        lax.psum_scatter(
            total_out.astype(jnp.bfloat16), "dp", scatter_dimension=0, tiled=True
        ).astype(jnp.float32),
        lax.psum_scatter(
            total_up.astype(jnp.bfloat16), "dp", scatter_dimension=0, tiled=True
        ).astype(jnp.float32),
        lax.psum_scatter(
            total_down.astype(jnp.bfloat16), "dp", scatter_dimension=0, tiled=True
        ).astype(jnp.float32),
    )
    section_edges = jnp.where(
        section_index == 0, edge_grads, outputs_mb * live_float[:, None, None]
    )
    return (
        section_edges[None, :, None],
        final[0][None],
        final[1][None],
        final[2][None],
        final[3][None],
        final[4][None],
        final[5][None],
        final[6][None],
    )


def solution(mesh):
    return jax.shard_map(
        shards,
        mesh=mesh,
        in_specs=(
            P("section", None, "dp", "seq", None),
            P(None, "dp"),
            P("section", None, "dp"),
            P("section", None, "dp"),
            P("section", "dp"),
            P("section", "dp", None),
            P("section", "dp", None),
            P("section", "dp", None),
            P("section", "dp", None),
        ),
        out_specs=(
            P("section", None, "dp", "seq", None),
            P("section", None, "dp"),
            P("section", None, "dp"),
            P("section", "dp"),
            P("section", "dp", None),
            P("section", "dp", None),
            P("section", "dp", None),
            P("section", "dp", None),
        ),
        check_vma=False,
    )
```

profile of v0, /device:TPU:0, one launch (start us, length us, event | category | flops | bytes accessed | tf_op | source)
XLA Modules:
  0.0 776.6 jit_solution(12875709357104750229)
XLA Ops:
  10.5 9.5 %all-gather = bf16[1,2,512]{2,1,0:T(2,128)(2,1)S(1)} all-gather(bf16[1,2,128]{2,1,0:T(2,128)(2,1)} %param.23), channel_id=2, replica_groups=mesh['section'=2,'dp'=4,'seq'=4] {'dp'}, dimensions={2}, use_global_device_ids=true | all-gather | bytes 2560 | tf_op jit(solution)/shard_map/all_gather | solution.py:266
  20.0 7.9 %all-gather.1 = bf16[1,6,512]{2,1,0:T(8,128)(2,1)S(1)} all-gather(bf16[1,6,128]{2,1,0:T(8,128)(2,1)} %param.24), channel_id=3, replica_groups=mesh['section'=2,'dp'=4,'seq'=4] {'dp'}, dimensions={2}, use_global_device_ids=true | all-gather | bytes 7680 | tf_op jit(solution)/shard_map/all_gather | solution.py:267
  31.5 12.1 %all-gather.11.cloned.1.call-done = bf16[1,512,1536]{2,1,0:T(8,128)(2,1)} async-done(((bf16[1,128,1536]{2,1,0:T(8,128)(2,1)}), bf16[1,512,1536]{2,1,0:T(8,128)(2,1)}) %all-gather.11.cloned.1.call-update) | async-done | bytes 1572880 | tf_op jit(solution)/shard_map/all_gather | solution.py:269
  53.0 25.0 %all-to-all-done = bf16[256,3,512]{0,1,2:T(4,128)(2,1)S(1)} async-done(((bf16[256,3,512]{0,1,2:T(4,128)(2,1)}), bf16[256,3,512]{0,1,2:T(4,128)(2,1)S(1)}, u32[]{:S(2)}, u32[]{:S(2)}) %all-to-all-start) | async-done | bytes 786464 | tf_op jit(solution)/shard_map/all_to_all | solution.py:158
  79.4 14.8 %while.84 = (s32[]{:T(128)}, bf16[2,512,2,64]{1,3,2,0:T(8,128)(2,1)S(1)}, f32[2,2,512]{2,1,0:T(2,128)S(1)}, s32[2]{0:T(128)S(1)}, bf16[1024,2,64]{0,2,1:T(8,128)...) while((s32[]{:T(128)}, ...), condition=%wide.region_5.6_spmd.clone, body=%wide.region_2.5_spmd.clone.sunk | while | flops 281607680 | bytes 15503531 | solution.py:86
  98.8 8.0 %all-gather.5 = bf16[1,2048]{1,0:T(2,128)(2,1)S(1)} all-gather(bf16[1,512]{1,0:T(2,128)(2,1)S(1)} %copy-done.87), channel_id=7, replica_groups=mesh['section'=2,'dp'=4,'seq'=4] {'dp'}, dimensions={1}, use_global_device_ids=true | all-gather | bytes 5120 | tf_op jit(solution)/shard_map/all_gather | solution.py:268
  106.8 13.8 %all-gather.3 = bf16[1,512,512]{2,1,0:T(8,128)(2,1)S(1)} all-gather(bf16[1,128,512]{2,1,0:T(8,128)(2,1)S(1)} %copy-done.68), channel_id=5, replica_groups=mesh['section'=2,'dp'=4,'seq'=4] {'dp'}, dimensions={1}, use_global_device_ids=true | all-gather | bytes 655360 | tf_op jit(solution)/shard_map/all_gather | solution.py:270
  146.7 23.0 %all-to-all-done.2 = bf16[256,3,512]{0,1,2:T(4,128)(2,1)S(1)} async-done(((bf16[256,3,512]{0,1,2:T(4,128)(2,1)}), bf16[256,3,512]{0,1,2:T(4,128)(2,1)S(1)}, u32[]{:S(2)}, u32[]{:S(2)}) %all-to-all-start.2) | async-done | bytes 786464 | tf_op jit(solution)/shard_map/all_to_all | solution.py:158
  172.0 14.8 %while.85 = (s32[]{:T(128)}, bf16[2,512,2,64]{1,3,2,0:T(8,128)(2,1)S(1)}, f32[2,2,512]{2,1,0:T(2,128)S(1)}, s32[2]{0:T(128)S(1)}, bf16[1024,2,64]{0,2,1:T(8,128)...) while((s32[]{:T(128)}, ...), condition=%wide.region_13.14_spmd.clone, body=%wide.region_10.13_spmd.clone.sunk | while | flops 281607680 | bytes 15503531 | solution.py:86
  230.4 17.9 %all-to-all-done.4 = bf16[256,3,512]{0,1,2:T(4,128)(2,1)} async-done(((bf16[256,3,512]{0,1,2:T(4,128)(2,1)}), bf16[256,3,512]{0,1,2:T(4,128)(2,1)}, u32[]{:S(2)}, u32[]{:S(2)}) %all-to-all-start.4) | async-done | bytes 786464 | tf_op jit(solution)/shard_map/all_to_all | solution.py:158
  260.7 18.3 %while.86 = (s32[]{:T(128)}, bf16[2,512,2,64]{1,3,2,0:T(8,128)(2,1)}, f32[2,2,512]{2,1,0:T(2,128)S(1)}, s32[2]{0:T(128)S(1)}, bf16[1024,2,64]{0,2,1:T(8,128)(2,1...) while((s32[]{:T(128)}, ...), condition=%wide.region_21.22_spmd.clone, body=%wide.region_18.21_spmd.clone.sunk | while | flops 281607680 | bytes 18649344 | solution.py:86
  289.9 7.5 all-to-all-done.5
  326.7 21.5 %while.87 = (s32[]{:T(128)}, f32[1024,2,64]{0,2,1:T(8,128)S(1)}, f32[1024,2,64]{0,2,1:T(8,128)}, bf16[2,512,2,64]{1,3,2,0:T(8,128)(2,1)S(1)}, s32[2]{0:T(128)S(1...) while((s32[]{:T(128)}, f32[1024,2,64]{0,2,1:T(8,128)S(1)}, ...), condition=%wide.region_32.33_spmd.clone, body=%wide.region_30.32_spmd.clone.sunk | while | flops 688061952 | bytes 41451792 | solution.py:141
  354.7 23.5 %all-to-all-done.7 = bf16[1024,3,128]{2,1,0:T(4,128)(2,1)S(1)} async-done(((bf16[1024,3,128]{2,1,0:T(4,128)(2,1)}), bf16[1024,3,128]{2,1,0:T(4,128)(2,1)S(1)}, u32[]{:S(2)}, u32[]{:S(2)}) %all-to-all-start.7) | async-done | bytes 786464 | tf_op jit(solution)/shard_map/all_to_all | solution.py:204
  419.4 23.0 %while.88 = (s32[]{:T(128)}, f32[1024,2,64]{0,2,1:T(8,128)S(1)}, f32[1024,2,64]{0,2,1:T(8,128)}, bf16[2,512,2,64]{1,3,2,0:T(8,128)(2,1)}, s32[2]{0:T(128)S(1)}, ...) while((s32[]{:T(128)}, f32[1024,2,64]{0,2,1:T(8,128)S(1)}, ...), condition=%wide.region_43.44_spmd.clone, body=%wide.region_41.43_spmd.clone.sunk | while | flops 688061952 | bytes 46694812 | solution.py:141
  462.1 18.8 %all-to-all-done.9 = bf16[1024,3,128]{2,1,0:T(4,128)(2,1)} async-done(((bf16[1024,3,128]{2,1,0:T(4,128)(2,1)}), bf16[1024,3,128]{2,1,0:T(4,128)(2,1)}, u32[]{:S(2)}, u32[]{:S(2)}) %all-to-all-start.9) | async-done | bytes 786464 | tf_op jit(solution)/shard_map/all_to_all | solution.py:204
  534.8 21.6 %while.89 = (s32[]{:T(128)}, f32[1024,2,64]{0,2,1:T(8,128)S(1)}, f32[1024,2,64]{0,2,1:T(8,128)}, bf16[2,512,2,64]{1,3,2,0:T(8,128)(2,1)S(1)}, s32[2]{0:T(128)S(1...) while((s32[]{:T(128)}, f32[1024,2,64]{0,2,1:T(8,128)S(1)}, ...), condition=%wide.region_54.55_spmd.clone, body=%wide.region_52.54_spmd.clone.sunk | while | flops 688061952 | bytes 41451792 | solution.py:141
  565.1 22.7 %all-to-all-done.11 = bf16[1024,3,128]{2,1,0:T(4,128)(2,1)S(1)} async-done(((bf16[1024,3,128]{2,1,0:T(4,128)(2,1)}), bf16[1024,3,128]{2,1,0:T(4,128)(2,1)S(1)}, u32[]{:S(2)}, u32[]{:S(2)}) %all-to-all-start.11) | async-done | bytes 786464 | tf_op jit(solution)/shard_map/all_to_all | solution.py:204
  611.8 23.1 %reduce-scatter.11.cloned.1.call-done = bf16[128,1536]{1,0:T(8,128)(2,1)} async-done(((bf16[512,1536]{1,0:T(8,128)(2,1)}), bf16[128,1536]{1,0:T(8,128)(2,1)}) %reduce-scatter.11.cloned.1.call-update) | async-done | bytes 393232 | tf_op jit(solution)/shard_map/reduce_scatter | solution.py:340
  635.0 8.9 %all-reduce = bf16[2048]{0:T(1024)(128)(2,1)S(1)} all-reduce(bf16[2048]{0:T(1024)(128)(2,1)S(1)} %add_convert_fusion.15), channel_id=11, replica_groups=mesh['section'=2,'dp'=4,'seq'=4] {'dp'}, use_global_device_ids=true, to_apply=%region_89.90.clone | all-reduce | flops 2048 | bytes 8192
  646.7 15.6 %reduce-scatter.19.cloned.1.call-done = bf16[128,2]{1,0:T(8,128)(2,1)} async-done(((bf16[512,2]{1,0:T(8,128)(2,1)}), bf16[128,2]{1,0:T(8,128)(2,1)}) %reduce-scatter.19.cloned.1.call-update) | async-done | bytes 528
  663.1 26.4 %reduce-scatter.21.cloned.1.call-done = bf16[128,6]{1,0:T(8,128)(2,1)} async-done(((bf16[512,6]{1,0:T(8,128)(2,1)}), bf16[128,6]{1,0:T(8,128)(2,1)}) %reduce-scatter.21.cloned.1.call-update) | async-done | bytes 1552
  690.3 11.8 %all-reduce.1 = (bf16[2,128]{1,0:T(2,128)(2,1)S(1)}, bf16[6,128]{1,0:T(8,128)(2,1)S(1)}, bf16[512]{0:T(512)(128)(2,1)S(1)}) all-reduce(bf16[2,128]{1,0:T(2,128)(2,1)S(1)} %copy.188, bf16[6,128]{1,0:T(8,128)(2,1)S(1)} %copy.190, bf16[512]{0:T(512)(128)(2,1)S(1)} %dynamic-slice.10), channel_id=1, replica_groups=mesh['section'=2,'dp'=4,'seq'=4] {'seq'}, use_global_device_ids=true, to_apply=%region_63.64 | all-reduce | flops 1536 | bytes 6144 | tf_op jit(solution)/shard_map/psum | solution.py:322
  703.8 58.6 %all-reduce.5.cloned.1.call-done = (bf16[128,1536]{1,0:T(8,128)(2,1)}, bf16[128,512]{1,0:T(8,128)(2,1)}, bf16[128,2048]{1,0:T(8,128)(2,1)}, bf16[512,512]{1,0:T(8,128)(2,1)}) async-done(((bf16[128,1536]{1,0:T(8,128)(2,1)}, bf16[128,512]{1,0:T(8,128)(2,1)}, bf16[128,2048]{1,0:T(8,128)(2,1)}, bf16[512,512]{1,0:T(8,128)(2,1)}), (bf16[128,1536]{1,0:T(8,128)(2,1)}, bf16[128,512]{1,0:T(8,128)(2,1)}, ...) | async-done | bytes 1572880 | tf_op jit(solution)/shard_map/psum | solution.py:325
  (641 shorter events, 401.6 us)
Async XLA Ops:
  7.2 36.4 %all-gather.11.cloned.1.call-start = ((), (), s32[]{:S(2)}) async-start(), calls=%async_computation.18 | async-start | bytes 1966080 | tf_op jit(solution)/shard_map/all_gather | solution.py:269
  7.9 113.4 %all-gather.13.cloned.1.call-start = ((), (), s32[]{:S(2)}) async-start(), calls=%async_computation.19 | async-start | bytes 2621440 | tf_op jit(solution)/shard_map/all_gather | solution.py:271
  47.7 30.3 %all-to-all-start = ((bf16[256,3,512]{0,1,2:T(4,128)(2,1)}), bf16[256,3,512]{0,1,2:T(4,128)(2,1)S(1)}, u32[]{:S(2)}, u32[]{:S(2)}) async-start(bf16[256,3,512]{0,1,2:T(4,128)(2,1)} %copy.139), calls=%async_computation | async-start | bytes 2097152 | tf_op jit(solution)/shard_map/all_to_all | solution.py:158
  52.3 74.5 %all-gather.15.cloned.1.call-start = ((), (), s32[]{:S(2)}) async-start(), calls=%async_computation.20 | async-start | bytes 2621440 | tf_op jit(solution)/shard_map/all_gather | solution.py:272
  95.4 25.3 %all-to-all-start.1 = ((bf16[4,256,128]{1,2,0:T(8,128)(2,1)}), bf16[4,256,128]{1,2,0:T(8,128)(2,1)S(1)}, u32[]{:S(2)}, u32[]{:S(2)}) async-start(bf16[4,256,128]{1,2,0:T(8,128)(2,1)} %copy.143), calls=%async_computation.1 | async-start | bytes 524288 | tf_op jit(solution)/shard_map/all_to_all | solution.py:166
  138.4 31.3 %all-to-all-start.2 = ((bf16[256,3,512]{0,1,2:T(4,128)(2,1)}), bf16[256,3,512]{0,1,2:T(4,128)(2,1)S(1)}, u32[]{:S(2)}, u32[]{:S(2)}) async-start(bf16[256,3,512]{0,1,2:T(4,128)(2,1)} %copy.145), calls=%async_computation.2 | async-start | bytes 2097152 | tf_op jit(solution)/shard_map/all_to_all | solution.py:158
  188.0 11.9 %all-to-all-start.3 = ((bf16[4,256,128]{1,2,0:T(8,128)(2,1)}), bf16[4,256,128]{1,2,0:T(8,128)(2,1)S(1)}, u32[]{:S(2)}, u32[]{:S(2)}) async-start(bf16[4,256,128]{1,2,0:T(8,128)(2,1)} %copy.149), calls=%async_computation.3 | async-start | bytes 524288 | tf_op jit(solution)/shard_map/all_to_all | solution.py:166
  217.5 30.8 %all-to-all-start.4 = ((bf16[256,3,512]{0,1,2:T(4,128)(2,1)}), bf16[256,3,512]{0,1,2:T(4,128)(2,1)}, u32[]{:S(2)}, u32[]{:S(2)}) async-start(bf16[256,3,512]{0,1,2:T(4,128)(2,1)} %copy.151), calls=%async_computation.4 | async-start | bytes 2097152 | tf_op jit(solution)/shard_map/all_to_all | solution.py:158
  284.4 13.0 %all-to-all-start.5 = ((bf16[4,256,128]{1,2,0:T(8,128)(2,1)}), bf16[4,256,128]{1,2,0:T(8,128)(2,1)}, u32[]{:S(2)}, u32[]{:S(2)}) async-start(bf16[4,256,128]{1,2,0:T(8,128)(2,1)} %copy.155), calls=%async_computation.5 | async-start | bytes 524288 | tf_op jit(solution)/shard_map/all_to_all | solution.py:166
  314.0 10.6 %all-to-all-start.6 = ((bf16[256,4,128]{2,0,1:T(8,128)(2,1)}), bf16[256,4,128]{2,0,1:T(8,128)(2,1)S(1)}, u32[]{:S(2)}, u32[]{:S(2)}) async-start(bf16[256,4,128]{2,0,1:T(8,128)(2,1)} %bitcast.903), calls=%async_computation.6 | async-start | bytes 524288 | tf_op jit(solution)/shard_map/all_to_all | solution.py:202
  350.8 27.5 %all-to-all-start.7 = ((bf16[1024,3,128]{2,1,0:T(4,128)(2,1)}), bf16[1024,3,128]{2,1,0:T(4,128)(2,1)S(1)}, u32[]{:S(2)}, u32[]{:S(2)}) async-start(bf16[1024,3,128]{2,1,0:T(4,128)(2,1)} %copy.163), calls=%async_computation.7 | async-start | bytes 2097152 | tf_op jit(solution)/shard_map/all_to_all | solution.py:204
  385.7 3.4 collective-permute-start.2
  399.9 15.2 %all-to-all-start.8 = ((bf16[256,4,128]{2,0,1:T(8,128)(2,1)}), bf16[256,4,128]{2,0,1:T(8,128)(2,1)}, u32[]{:S(2)}, u32[]{:S(2)}) async-start(bf16[256,4,128]{2,0,1:T(8,128)(2,1)} %bitcast.902), calls=%async_computation.8 | async-start | bytes 524288 | tf_op jit(solution)/shard_map/all_to_all | solution.py:202
  449.9 31.0 %all-to-all-start.9 = ((bf16[1024,3,128]{2,1,0:T(4,128)(2,1)}), bf16[1024,3,128]{2,1,0:T(4,128)(2,1)}, u32[]{:S(2)}, u32[]{:S(2)}) async-start(bf16[1024,3,128]{2,1,0:T(4,128)(2,1)} %copy.170), calls=%async_computation.9 | async-start | bytes 2097152 | tf_op jit(solution)/shard_map/all_to_all | solution.py:204
  455.1 156.7 %reduce-scatter.13.cloned.1.call-start = ((), (), s32[]{:S(2)}) async-start(), calls=%async_computation.22 | async-start | bytes 655360 | tf_op jit(solution)/shard_map/reduce_scatter | solution.py:343
  489.2 3.5 collective-permute-start.3
  501.1 110.7 %reduce-scatter.15.cloned.1.call-start = ((), (), s32[]{:S(2)}) async-start(), calls=%async_computation.23 | async-start | bytes 2621440 | tf_op jit(solution)/shard_map/reduce_scatter | solution.py:346
  521.3 13.0 %all-to-all-start.10 = ((bf16[256,4,128]{2,0,1:T(8,128)(2,1)}), bf16[256,4,128]{2,0,1:T(8,128)(2,1)S(1)}, u32[]{:S(2)}, u32[]{:S(2)}) async-start(bf16[256,4,128]{2,0,1:T(8,128)(2,1)} %bitcast.778), calls=%async_computation.10 | async-start | bytes 524288 | tf_op jit(solution)/shard_map/all_to_all | solution.py:202
  524.7 87.0 %reduce-scatter.17.cloned.1.call-start = ((), (), s32[]{:S(2)}) async-start(), calls=%async_computation.24 | async-start | bytes 2621440 | tf_op jit(solution)/shard_map/reduce_scatter | solution.py:349
  559.0 28.8 %all-to-all-start.11 = ((bf16[1024,3,128]{2,1,0:T(4,128)(2,1)}), bf16[1024,3,128]{2,1,0:T(4,128)(2,1)S(1)}, u32[]{:S(2)}, u32[]{:S(2)}) async-start(bf16[1024,3,128]{2,1,0:T(4,128)(2,1)} %copy.177), calls=%async_computation.11 | async-start | bytes 2097152 | tf_op jit(solution)/shard_map/all_to_all | solution.py:204
  562.6 72.3 %reduce-scatter.11.cloned.1.call-start = ((), (), s32[]{:S(2)}) async-start(), calls=%async_computation.21 | async-start | bytes 1966080 | tf_op jit(solution)/shard_map/reduce_scatter | solution.py:340
  595.0 67.3 %reduce-scatter.19.cloned.1.call-start = ((), (), s32[]{:S(2)}) async-start(), calls=%async_computation.25 | async-start | bytes 163840
  609.9 79.6 %reduce-scatter.21.cloned.1.call-start = ((), (), s32[]{:S(2)}) async-start(), calls=%async_computation.26 | async-start | bytes 163840
  610.9 151.5 %all-reduce.5.cloned.1.call-start = ((), (), s32[]{:S(2)}) async-start(), calls=%async_computation.27 | async-start | bytes 3145728 | tf_op jit(solution)/shard_map/psum | solution.py:325
  (119 other events, 950.1 us)
Sparse Core Ops, SparseCore 0:
  9.8 33.6 all-gather.10
  45.4 35.2 all-gather.12
  82.6 39.6 all-gather.14
  501.2 23.0 reduce-scatter.12
  527.4 35.1 reduce-scatter.14
  565.4 35.1 reduce-scatter.16
  603.9 30.9 reduce-scatter.10
  638.4 23.8 reduce-scatter.18
  665.6 23.8 reduce-scatter.20
  692.2 70.2 all-reduce.4
where the time goes:
time: 788 us; the launch traced here: 777 us
  waiting for transfers between devices  289 us (37%)
  matrix products  135 us (17%)
  local copies, waits for them, and re-layouts  123 us (16%)
  other arithmetic  74 us (9%)
  blocking collectives  59.9 us (8%)
  starting transfers between devices  55.5 us (7%)
  loops' own time  23.7 us (3%)
  between operations  17 us (2%)
    all_to_all x3, waiting for transfers between devices, section_forward(): lax.all_to_all(qkv_tokens.reshape(row_count, 3, model_width), 'seq', spli...  65.9 us
    all_to_all x3, waiting for transfers between devices, section_backward(): lax.all_to_all(grad_packed_heads, 'seq', split_axis=0, concat_axis=2, til...  65.1 us
    psum x1, waiting for transfers between devices, shards(): lax.psum(sum_qkv.astype(jnp.bfloat16), 'seq').astype(jnp.float32)  58.6 us
    unnamed x12, waiting for transfers between devices  44.2 us
    dot_general x12, matrix products, dot_first(): lax.dot_general(left, right, (((0,), (0,)), ((), ())), preferred_element_...  31.6 us
    dot_general x12, matrix products, dot_last(): lax.dot_general(left, right, (((1,), (1,)), ((), ())), preferred_element_...  24.9 us
    dot_general x12, matrix products, matmul(): return jnp.dot(left, right, preferred_element_type=jnp.float32)  24.4 us
    reduce_scatter x1, waiting for transfers between devices, shards(): lax.psum_scatter(total_qkv.astype(jnp.bfloat16), 'dp', scatter_dimension=...  23.1 us
  transfers between devices with their start and end apart: 26, of which 19 were waited for; matrix products, arithmetic and copies ran while one was open for 19% of the time, Pallas kernels for 0%

commit v1 on v0

--- a/solution.py
+++ b/solution.py
@@ -7,12 +7,6 @@
 
 
 EPSILON = 1e-05
-
-
-def from_behind(block, axis, distance):
-    devices = range(lax.axis_size(axis))
-    route = [(i - distance, i) for i in devices if i - distance in devices]
-    return lax.ppermute(block, axis, route)
 
 
 def layer_norm(values, gain, shift):
@@ -239,10 +233,31 @@
     )
 
 
-def store(buffer_rows, value, place, is_valid):
-    previous = lax.dynamic_index_in_dim(buffer_rows, place, 0, keepdims=False)
-    chosen = jnp.where(is_valid, value, previous)
-    return lax.dynamic_update_index_in_dim(buffer_rows, chosen, place, 0)
+def swap_cores(block):
+    return lax.ppermute(block, "section", [(0, 1), (1, 0)])
+
+
+def pack_small(gains, shifts, bias):
+    pieces = lax.axis_size("dp")
+    return jnp.concatenate(
+        [
+            jnp.moveaxis(gains.reshape(gains.shape[0], pieces, -1), 1, 0).reshape(pieces, -1),
+            jnp.moveaxis(shifts.reshape(shifts.shape[0], pieces, -1), 1, 0).reshape(pieces, -1),
+            bias.reshape(pieces, -1),
+        ],
+        axis=1,
+    )
+
+
+def half_sum(grad, is_first, after=None):
+    half = grad.shape[1] // 2
+    low, high = grad[:, :half], grad[:, half:]
+    away = jnp.where(is_first, high, low).astype(jnp.bfloat16)
+    total = jnp.where(is_first, low, high) + swap_cores(away).astype(jnp.float32)
+    own_rows = lax.psum_scatter(total.astype(jnp.bfloat16), "dp", scatter_dimension=0, tiled=True)
+    if after is not None:
+        own_rows = lax.optimization_barrier((own_rows, after))[0]
+    return lax.psum(own_rows, "seq")
 
 
 def shards(
@@ -256,113 +271,81 @@
     expand_weight,
     contract_weight,
 ):
-    section_index = lax.axis_index("section")
-    micro_count = section_ends.shape[1]
+    core = lax.axis_index("section")
+    is_first = core == 0
     local_ends = section_ends[0, :, 0]
-    row_count = local_ends.shape[1]
-    model_width = local_ends.shape[2]
     live_float = live[:, 0].astype(jnp.float32)
-    weights = (
-        lax.all_gather(norm_gains[0], "dp", axis=1, tiled=True),
-        lax.all_gather(offsets[0], "dp", axis=1, tiled=True),
-        lax.all_gather(expand_bias[0], "dp", axis=0, tiled=True),
-        lax.all_gather(query_key_value[0], "dp", axis=0, tiled=True),
-        lax.all_gather(attention_out[0], "dp", axis=0, tiled=True),
-        lax.all_gather(expand_weight[0], "dp", axis=0, tiled=True),
-        lax.all_gather(contract_weight[0], "dp", axis=0, tiled=True),
-    )
-    incoming = jnp.zeros((row_count, model_width), jnp.bfloat16)
-    buffers = None
-    outputs_mb = jnp.zeros((micro_count, row_count, model_width), jnp.float32)
-    for step_number in range(micro_count + 1):
-        index_mb = step_number - section_index
-        is_valid = (index_mb >= 0) & (index_mb < micro_count)
-        safe_index = jnp.clip(index_mb, 0, micro_count - 1)
-        own_input = lax.dynamic_index_in_dim(local_ends, safe_index, 0, keepdims=False)
-        tokens_low = jnp.where(section_index == 0, own_input, incoming)
-        result, saved = section_forward(tokens_low.astype(jnp.float32), weights)
-        record = (tokens_low,) + saved
-        if buffers is None:
-            buffers = tuple((jnp.zeros((micro_count,) + a.shape, a.dtype) for a in record))
-        buffers = tuple((store(a, b, safe_index, is_valid) for a, b in zip(buffers, record)))
-        outputs_mb = store(outputs_mb, result, safe_index, is_valid)
-        if step_number < micro_count:
-            incoming = from_behind(result.astype(jnp.bfloat16), "section", 1)
-    weights_back = (
-        lax.all_gather(norm_gains[0], "dp", axis=1, tiled=True),
-        lax.all_gather(offsets[0], "dp", axis=1, tiled=True),
-        lax.all_gather(expand_bias[0], "dp", axis=0, tiled=True),
-        lax.all_gather(query_key_value[0], "dp", axis=0, tiled=True),
-        lax.all_gather(attention_out[0], "dp", axis=0, tiled=True),
-        lax.all_gather(expand_weight[0], "dp", axis=0, tiled=True),
-        lax.all_gather(contract_weight[0], "dp", axis=0, tiled=True),
-    )
-    grad_sums = tuple((jnp.zeros(a.shape, jnp.float32) for a in weights_back))
-    edge_grads = jnp.zeros((micro_count, row_count, model_width), jnp.float32)
-    arriving = jnp.zeros((row_count, model_width), jnp.bfloat16)
-    for step_number in range(micro_count + 1):
-        index_mb = step_number - 1 + section_index
-        is_valid = (index_mb >= 0) & (index_mb < micro_count)
-        safe_index = jnp.clip(index_mb, 0, micro_count - 1)
-        own_cotangent = lax.dynamic_index_in_dim(local_ends, safe_index, 0, keepdims=False).astype(
-            jnp.float32
-        )
-        own_cotangent = own_cotangent * lax.dynamic_index_in_dim(
-            live_float, safe_index, 0, keepdims=False
-        )
-        grad_out = jnp.where(section_index == 1, own_cotangent, arriving.astype(jnp.float32))
-        saved = tuple((lax.dynamic_index_in_dim(a, safe_index, 0, keepdims=False) for a in buffers))
-        grad_tokens, grads = section_backward(grad_out, saved, weights_back)
-        grad_sums = tuple((a + jnp.where(is_valid, b, 0.0) for a, b in zip(grad_sums, grads)))
-        edge_grads = store(edge_grads, grad_tokens, safe_index, is_valid)
-        if step_number < micro_count:
-            arriving = from_behind(grad_tokens.astype(jnp.bfloat16), "section", -1)
-    sum_gains, sum_shifts, sum_bias, sum_qkv, sum_out, sum_up, sum_down = grad_sums
-    total_gains, total_shifts, total_bias, total_qkv, total_out, total_up, total_down = (
-        lax.psum(sum_gains.astype(jnp.bfloat16), "seq").astype(jnp.float32),
-        lax.psum(sum_shifts.astype(jnp.bfloat16), "seq").astype(jnp.float32),
-        lax.psum(sum_bias.astype(jnp.bfloat16), "seq").astype(jnp.float32),
-        lax.psum(sum_qkv.astype(jnp.bfloat16), "seq").astype(jnp.float32),
-        lax.psum(sum_out.astype(jnp.bfloat16), "seq").astype(jnp.float32),
-        lax.psum(sum_up.astype(jnp.bfloat16), "seq").astype(jnp.float32),
-        lax.psum(sum_down.astype(jnp.bfloat16), "seq").astype(jnp.float32),
-    )
-    final = (
-        lax.psum_scatter(
-            total_gains.astype(jnp.bfloat16), "dp", scatter_dimension=1, tiled=True
-        ).astype(jnp.float32),
-        lax.psum_scatter(
-            total_shifts.astype(jnp.bfloat16), "dp", scatter_dimension=1, tiled=True
-        ).astype(jnp.float32),
-        lax.psum_scatter(
-            total_bias.astype(jnp.bfloat16), "dp", scatter_dimension=0, tiled=True
-        ).astype(jnp.float32),
-        lax.psum_scatter(
-            total_qkv.astype(jnp.bfloat16), "dp", scatter_dimension=0, tiled=True
-        ).astype(jnp.float32),
-        lax.psum_scatter(
-            total_out.astype(jnp.bfloat16), "dp", scatter_dimension=0, tiled=True
-        ).astype(jnp.float32),
-        lax.psum_scatter(
-            total_up.astype(jnp.bfloat16), "dp", scatter_dimension=0, tiled=True
-        ).astype(jnp.float32),
-        lax.psum_scatter(
-            total_down.astype(jnp.bfloat16), "dp", scatter_dimension=0, tiled=True
-        ).astype(jnp.float32),
-    )
-    section_edges = jnp.where(
-        section_index == 0, edge_grads, outputs_mb * live_float[:, None, None]
-    )
-    return (
-        section_edges[None, :, None],
-        final[0][None],
-        final[1][None],
-        final[2][None],
-        final[3][None],
-        final[4][None],
-        final[5][None],
-        final[6][None],
-    )
+    gain_size, shift_size, bias_size = norm_gains[0].size, offsets[0].size, expand_bias[0].size
+    width = norm_gains.shape[2]
+
+    kept = jnp.where(is_first, local_ends[0], local_ends[1])
+    came = swap_cores(jnp.where(is_first, local_ends[1], local_ends[0]))
+    tokens_first = jnp.where(is_first, kept, came)
+    own_live = jnp.where(is_first, live_float[0], live_float[1])
+    cotangent = jnp.where(is_first, came, kept).astype(jnp.float32) * own_live
+
+    small = jnp.concatenate(
+        [norm_gains[0].reshape(-1), offsets[0].reshape(-1), expand_bias[0].reshape(-1)]
+    )
+    small = lax.all_gather(small[None], "dp", axis=0, tiled=True)
+    pieces = small.shape[0]
+    gathered = [small] + [
+        lax.all_gather(a[0], "dp", axis=0, tiled=True)
+        for a in (query_key_value, attention_out, expand_weight, contract_weight)
+    ]
+    others = [swap_cores(a) for a in gathered]
+
+    def layer_weights(chosen):
+        low = chosen[0]
+        gains = jnp.moveaxis(low[:, :gain_size].reshape(pieces, 2, width), 0, 1).reshape(2, -1)
+        shifts = jnp.moveaxis(
+            low[:, gain_size : gain_size + shift_size].reshape(pieces, 6, width), 0, 1
+        ).reshape(6, -1)
+        bias = low[:, gain_size + shift_size :].reshape(-1)
+        return (gains, shifts, bias) + tuple(chosen[1:])
+
+    weights_zero = layer_weights([jnp.where(is_first, a, b) for a, b in zip(gathered, others)])
+    weights_one = layer_weights([jnp.where(is_first, b, a) for a, b in zip(gathered, others)])
+
+    middle, saved_zero = section_forward(tokens_first.astype(jnp.float32), weights_zero)
+    tokens_second = middle.astype(jnp.bfloat16)
+    result, saved_one = section_forward(tokens_second.astype(jnp.float32), weights_one)
+    grad_middle, grads_one = section_backward(
+        cotangent, (tokens_second,) + saved_one, weights_one
+    )
+    halves_one = [half_sum(g, is_first) for g in grads_one[3:]]
+    grad_middle = grad_middle.astype(jnp.bfloat16).astype(jnp.float32)
+    grad_first, grads_zero = section_backward(
+        grad_middle, (tokens_first,) + saved_zero, weights_zero
+    )
+    halves_zero = [half_sum(g, is_first, halves_one) for g in grads_zero[3:]]
+
+    small_zero, small_one = pack_small(*grads_zero[:3]), pack_small(*grads_one[:3])
+    small_sum = jnp.where(is_first, small_zero, small_one) + swap_cores(
+        jnp.where(is_first, small_one, small_zero)
+    )
+    small_sum = lax.psum(
+        lax.psum_scatter(small_sum, "dp", scatter_dimension=0, tiled=True), "seq"
+    )[0]
+    final_small = (
+        small_sum[:gain_size].reshape(1, 2, width),
+        small_sum[gain_size : gain_size + shift_size].reshape(1, 6, width),
+        small_sum[gain_size + shift_size :].reshape(1, bias_size),
+    )
+
+    final_large = []
+    for zero, one in zip(halves_zero, halves_one):
+        mine = jnp.where(is_first, zero, one)
+        arrived = swap_cores(jnp.where(is_first, one, zero))
+        left = jnp.where(is_first, mine, arrived)
+        right = jnp.where(is_first, arrived, mine)
+        final_large.append(jnp.concatenate([left, right], axis=1).astype(jnp.float32)[None])
+
+    result = result * own_live
+    stays = jnp.where(is_first, grad_first, result)
+    comes = swap_cores(jnp.where(is_first, result, grad_first))
+    edges = jnp.stack([jnp.where(is_first, stays, comes), jnp.where(is_first, comes, stays)])
+    return (edges[None, :, None],) + final_small + tuple(final_large)
 
 
 def solution(mesh):

time: 788 us -> 631 us (0.80)
  local copies, waits for them, and re-layouts: 123 us -> 44.6 us
  matrix products: 135 us -> 99.8 us
  starting transfers between devices: 55.5 us -> 43.4 us
  blocking collectives: 59.9 us -> 49.1 us
  other arithmetic: 74 us -> 64.8 us
  loops' own time: 23.7 us -> 15.8 us
    all_gather x3, waiting for transfers between devices: 12.1 us -> 71.1 us  [shards(): lax.all_gather(a[0], 'dp', axis=0, tiled=True)]
    reduce_scatter x4 -> x8, waiting for transfers between devices: 23.1 us -> 69.3 us  [half_sum(): lax.psum_scatter(total.astype(jnp.bfloat16), 'dp', scatter_dimension=0, t...]
    unnamed x12 -> x13, waiting for transfers between devices: 44.2 us -> 1.56 us
    all_to_all x3 -> x2, waiting for transfers between devices: 65.9 us -> 26.4 us  [section_forward(): lax.all_to_all(qkv_tokens.reshape(row_count, 3, model_width), 'seq', spli...]
    convert_element_type x6 -> x22, other arithmetic: 2.26 us -> 36 us  [the longest x8 21 us: half_sum(): total.astype(jnp.bfloat16)]
    psum x1 -> x2, waiting for transfers between devices: 58.6 us -> 31.8 us  [half_sum(): return lax.psum(own_rows, 'seq')]
    dynamic_slice x15 -> x0, local copies, waits for them, and re-layouts: 18.7 us -> none  [the longest x10 9.75 us: store(): previous = lax.dynamic_index_in_dim(buffer_rows, place, 0, keepdims=False)]
    dot_general x12 -> x8, matrix products: 31.6 us -> 13.9 us  [dot_first(): lax.dot_general(left, right, (((0,), (0,)), ((), ())), preferred_element_...]
  transfers between devices with their start and end apart: 26 -> 41, of which waited for: 19 -> 18; matrix products, arithmetic and copies ran while one was open for 19% -> 25% of each run, Pallas kernels for 0% -> 0%
where the time goes in v1:
time: 631 us; the launch traced here: 622 us
  waiting for transfers between devices  288 us (46%)
  matrix products  99.8 us (16%)
  other arithmetic  64.8 us (10%)
  blocking collectives  49.1 us (8%)
  local copies, waits for them, and re-layouts  44.6 us (7%)
  starting transfers between devices  43.4 us (7%)
  between operations  17 us (3%)
  loops' own time  15.8 us (3%)
    all_gather x3, waiting for transfers between devices, shards(): lax.all_gather(a[0], 'dp', axis=0, tiled=True)  71.1 us
    reduce_scatter x8, waiting for transfers between devices, half_sum(): lax.psum_scatter(total.astype(jnp.bfloat16), 'dp', scatter_dimension=0, t...  69.3 us
    all_to_all x2, waiting for transfers between devices, section_backward(): lax.all_to_all(grad_packed_heads, 'seq', split_axis=0, concat_axis=2, til...  57.6 us
    psum x2, waiting for transfers between devices, half_sum(): return lax.psum(own_rows, 'seq')  31.8 us
    all_to_all x2, waiting for transfers between devices, section_forward(): lax.all_to_all(qkv_tokens.reshape(row_count, 3, model_width), 'seq', spli...  26.4 us
    convert_element_type x8, other arithmetic, half_sum(): total.astype(jnp.bfloat16)  21 us
    all_to_all x2, waiting for transfers between devices, section_forward(): lax.all_to_all(attended_heads, 'seq', split_axis=0, concat_axis=1, tiled=...  18.3 us
    dot_general x8, matrix products, dot_last(): lax.dot_general(left, right, (((1,), (1,)), ((), ())), preferred_element_...  18.1 us
  transfers between devices with their start and end apart: 41, of which 18 were waited for; matrix products, arithmetic and copies ran while one was open for 25% of the time, Pallas kernels for 0%

profile of v1, /device:TPU:0, one launch (start us, length us, event | category | flops | bytes accessed | tf_op | source)
XLA Modules:
  0.0 622.4 jit_solution(15140490677537040493)
XLA Ops:
  10.1 9.6 %all-gather.5 = bf16[4,1,1536]{2,1,0:T(2,128)(2,1)S(1)} all-gather(bf16[1,1,1536]{2,1,0:T(2,128)(2,1)S(1)} %reshape.637), channel_id=2, replica_groups=mesh['section'=2,'dp'=4,'seq'=4] {'dp'}, dimensions={0}, use_global_device_ids=true | all-gather | bytes 15360 | tf_op jit(solution)/shard_map/all_gather | solution.py:290
  23.5 20.1 %all-gather.10.cloned.1.call-done = bf16[1,512,1536]{2,1,0:T(8,128)(2,1)} async-done(((bf16[1,128,1536]{2,1,0:T(8,128)(2,1)}), bf16[1,512,1536]{2,1,0:T(8,128)(2,1)}) %all-gather.10.cloned.1.call-update) | async-done | bytes 1572880 | tf_op jit(solution)/shard_map/all_gather | solution.py:293
  56.0 12.0 %all-gather.2 = bf16[1,512,512]{2,1,0:T(8,128)(2,1)S(1)} all-gather(bf16[1,128,512]{2,1,0:T(8,128)(2,1)S(1)} %copy-done.60), channel_id=4, replica_groups=mesh['section'=2,'dp'=4,'seq'=4] {'dp'}, dimensions={1}, use_global_device_ids=true | all-gather | bytes 655360 | tf_op jit(solution)/shard_map/all_gather | solution.py:293
  68.0 13.8 %all-gather.12.cloned.1.call-done = bf16[1,512,2048]{2,1,0:T(8,128)(2,1)} async-done(((bf16[1,128,2048]{2,1,0:T(8,128)(2,1)}), bf16[1,512,2048]{2,1,0:T(8,128)(2,1)}) %all-gather.12.cloned.1.call-update) | async-done | bytes 2097168 | tf_op jit(solution)/shard_map/all_gather | solution.py:293
  81.8 37.2 %all-gather.14.cloned.1.call-done = bf16[1,2048,512]{2,1,0:T(8,128)(2,1)} async-done(((bf16[1,512,512]{2,1,0:T(8,128)(2,1)}), bf16[1,2048,512]{2,1,0:T(8,128)(2,1)}) %all-gather.14.cloned.1.call-update) | async-done | bytes 2097168 | tf_op jit(solution)/shard_map/all_gather | solution.py:293
  121.1 16.6 %while.56 = (s32[]{:T(128)}, bf16[2,512,2,64]{1,3,2,0:T(8,128)(2,1)S(1)}, f32[2,2,512]{2,1,0:T(2,128)S(1)}, s32[2]{0:T(128)S(1)}, bf16[1024,2,64]{0,2,1:T(8,128)...) while((s32[]{:T(128)}, ...), condition=%wide.region_5.6_spmd.clone, body=%wide.region_2.5_spmd.clone.sunk | while | flops 281607680 | bytes 15503523 | solution.py:80
  142.9 5.1 all-to-all-start.1
  148.1 9.6 %all-to-all-done.1 = bf16[4,256,128]{1,2,0:T(8,128)(2,1)} async-done(((bf16[4,256,128]{1,2,0:T(8,128)(2,1)}), bf16[4,256,128]{1,2,0:T(8,128)(2,1)}, u32[]{:S(2)}, u32[]{:S(2)}) %all-to-all-start.1) | async-done | bytes 262176 | tf_op jit(solution)/shard_map/all_to_all | solution.py:160
  169.9 26.4 %all-to-all-done.2 = bf16[256,3,512]{0,1,2:T(4,128)(2,1)S(1)} async-done(((bf16[256,3,512]{0,1,2:T(4,128)(2,1)}), bf16[256,3,512]{0,1,2:T(4,128)(2,1)S(1)}, u32[]{:S(2)}, u32[]{:S(2)}) %all-to-all-start.2) | async-done | bytes 786464 | tf_op jit(solution)/shard_map/all_to_all | solution.py:152
  198.4 16.6 %while.57 = (s32[]{:T(128)}, bf16[2,512,2,64]{1,3,2,0:T(8,128)(2,1)S(1)}, f32[2,2,512]{2,1,0:T(2,128)S(1)}, s32[2]{0:T(128)S(1)}, bf16[1024,2,64]{0,2,1:T(8,128)...) while((s32[]{:T(128)}, ...), condition=%wide.region_13.14_spmd.clone, body=%wide.region_10.13_spmd.clone.sunk | while | flops 281607680 | bytes 15503523 | solution.py:80
  219.8 8.7 %all-to-all-done.3 = bf16[4,256,128]{1,2,0:T(8,128)(2,1)S(1)} async-done(((bf16[4,256,128]{1,2,0:T(8,128)(2,1)}), bf16[4,256,128]{1,2,0:T(8,128)(2,1)S(1)}, u32[]{:S(2)}, u32[]{:S(2)}) %all-to-all-start.3) | async-done | bytes 262176 | tf_op jit(solution)/shard_map/all_to_all | solution.py:160
  268.2 30.0 %while.58 = (s32[]{:T(128)}, f32[1024,2,64]{0,2,1:T(8,128)S(1)}, f32[1024,2,64]{0,2,1:T(8,128)}, bf16[2,512,2,64]{1,3,2,0:T(8,128)(2,1)}, s32[2]{0:T(128)S(1)}, ...) while((s32[]{:T(128)}, f32[1024,2,64]{0,2,1:T(8,128)S(1)}, ...), condition=%wide.region_20.21_spmd.clone, body=%wide.region_18.20_spmd.clone.sunk | while | flops 688061952 | bytes 76054944 | solution.py:135
  302.3 5.0 all-to-all-start.5
  311.8 21.9 %all-to-all-done.5 = bf16[1024,3,128]{2,1,0:T(4,128)(2,1)S(1)} async-done(((bf16[1024,3,128]{2,1,0:T(4,128)(2,1)}), bf16[1024,3,128]{2,1,0:T(4,128)(2,1)S(1)}, u32[]{:S(2)}, u32[]{:S(2)}) %all-to-all-start.5) | async-done | bytes 786464 | tf_op jit(solution)/shard_map/all_to_all | solution.py:198
  359.2 16.5 %reduce-scatter.11.cloned.1.call-done = bf16[128,768]{1,0:T(8,128)(2,1)} async-done(((bf16[512,768]{1,0:T(8,128)(2,1)}), bf16[128,768]{1,0:T(8,128)(2,1)}) %reduce-scatter.11.cloned.1.call-update) | async-done | bytes 196624 | tf_op jit(solution)/shard_map/reduce_scatter | solution.py:257
  376.8 4.6 all-to-all-start.6
  384.5 6.8 %all-to-all-done.6 = bf16[256,4,128]{2,0,1:T(8,128)(2,1)S(1)} async-done(((bf16[256,4,128]{2,0,1:T(8,128)(2,1)}), bf16[256,4,128]{2,0,1:T(8,128)(2,1)S(1)}, u32[]{:S(2)}, u32[]{:S(2)}) %all-to-all-start.6) | async-done | bytes 262176 | tf_op jit(solution)/shard_map/all_to_all | solution.py:196
  396.4 30.2 %while.59 = (s32[]{:T(128)}, f32[1024,2,64]{0,2,1:T(8,128)S(1)}, f32[1024,2,64]{0,2,1:T(8,128)}, bf16[2,512,2,64]{1,3,2,0:T(8,128)(2,1)}, s32[2]{0:T(128)S(1)}, ...) while((s32[]{:T(128)}, f32[1024,2,64]{0,2,1:T(8,128)S(1)}, ...), condition=%wide.region_27.28_spmd.clone, body=%wide.region_25.27_spmd.clone.sunk | while | flops 688061952 | bytes 76054944 | solution.py:135
  438.6 35.7 %all-to-all-done.7 = bf16[1024,3,128]{2,1,0:T(4,128)(2,1)} async-done(((bf16[1024,3,128]{2,1,0:T(4,128)(2,1)}), bf16[1024,3,128]{2,1,0:T(4,128)(2,1)}, u32[]{:S(2)}, u32[]{:S(2)}) %all-to-all-start.7) | async-done | bytes 786464 | tf_op jit(solution)/shard_map/all_to_all | solution.py:198
  491.2 15.6 %all-reduce = f32[4,1536]{1,0:T(4,128)S(1)} all-reduce(f32[4,1536]{1,0:T(4,128)S(1)} %select_add_fusion), channel_id=7, replica_groups=mesh['section'=2,'dp'=4,'seq'=4] {'dp'}, use_global_device_ids=true, to_apply=%region_48.49.clone | all-reduce | flops 6144 | bytes 49152
  506.9 23.3 %reduce-scatter.19.cloned.1.call-done = bf16[128,256]{1,0:T(8,128)(2,1)} async-done(((bf16[512,256]{1,0:T(8,128)(2,1)}), bf16[128,256]{1,0:T(8,128)(2,1)}) %reduce-scatter.19.cloned.1.call-update) | async-done | bytes 65552 | tf_op jit(solution)/shard_map/reduce_scatter | solution.py:257
  530.1 29.5 %reduce-scatter.9.cloned.1.call-done = bf16[128,768]{1,0:T(8,128)(2,1)} async-done(((bf16[512,768]{1,0:T(8,128)(2,1)}), bf16[128,768]{1,0:T(8,128)(2,1)}) %reduce-scatter.9.cloned.1.call-update) | async-done | bytes 196624 | tf_op jit(solution)/shard_map/reduce_scatter | solution.py:257
  560.3 11.9 %psum.63 = f32[1,1536]{1,0:T(1,128)S(1)} all-reduce(f32[1,1536]{1,0:T(1,128)S(1)} %constant_dynamic-slice_fusion), channel_id=1, replica_groups=mesh['section'=2,'dp'=4,'seq'=4] {'seq'}, use_global_device_ids=true, to_apply=%region_49.50 | all-reduce | flops 1536 | bytes 12288 | tf_op jit(solution)/shard_map/psum | solution.py:327
  575.1 31.8 %all-reduce.6.cloned.1.call-done = (bf16[128,768]{1,0:T(8,128)(2,1)}, bf16[128,256]{1,0:T(8,128)(2,1)}, bf16[128,1024]{1,0:T(8,128)(2,1)}, bf16[512,256]{1,0:T(8,128)(2,1)}) async-done(((bf16[128,768]{1,0:T(8,128)(2,1)}, bf16[128,256]{1,0:T(8,128)(2,1)}, bf16[128,1024]{1,0:T(8,128)(2,1)}, bf16[512,256]{1,0:T(8,128)(2,1)}), (bf16[128,768]{1,0:T(8,128)(2,1)}, bf16[128,256]{1,0:T(8,128)(2,1)}, ...) | async-done | bytes 786448 | tf_op jit(solution)/shard_map/psum | solution.py:260
  (516 shorter events, 244.5 us)
Async XLA Ops:
  7.2 36.4 %all-gather.10.cloned.1.call-start = ((), (), s32[]{:S(2)}) async-start(), calls=%async_computation.24 | async-start | bytes 1966080 | tf_op jit(solution)/shard_map/all_gather | solution.py:293
  7.9 73.9 %all-gather.12.cloned.1.call-start = ((), (), s32[]{:S(2)}) async-start(), calls=%async_computation.25 | async-start | bytes 2621440 | tf_op jit(solution)/shard_map/all_gather | solution.py:293
  8.7 110.4 %all-gather.14.cloned.1.call-start = ((), (), s32[]{:S(2)}) async-start(), calls=%async_computation.26 | async-start | bytes 2621440 | tf_op jit(solution)/shard_map/all_gather | solution.py:293
  20.9 23.3 %collective-permute-start = (bf16[256,512]{1,0:T(8,128)(2,1)S(1)}, bf16[256,512]{1,0:T(8,128)(2,1)S(1)}, u32[]{:S(2)}, u32[]{:S(2)}) collective-permute-start(bf16[256,512]{1,0:T(8,128)(2,1)S(1)} %select_bitcast_fusion.6), channel_id=1, source_target_pairs={{0,16},{16,0},{1,17},{17,1},{2,18},{18,2},{3,19},{19,3},{4,20},{20... | collective-permute-start | bytes 786440 | tf_op jit(solution)/shard_map/ppermute | solution.py:237
  51.4 67.7 %all-to-all-start = ((bf16[256,3,512]{0,1,2:T(4,128)(2,1)}), bf16[256,3,512]{0,1,2:T(4,128)(2,1)S(1)}, u32[]{:S(2)}, u32[]{:S(2)}) async-start(bf16[256,3,512]{0,1,2:T(4,128)(2,1)} %copy.75), calls=%async_computation | async-start | bytes 2097152 | tf_op jit(solution)/shard_map/all_to_all | solution.py:152
  68.0 80.1 %collective-permute-start.3 = (bf16[512,512]{1,0:T(8,128)(2,1)S(1)}, bf16[512,512]{1,0:T(8,128)(2,1)}, u32[]{:S(2)}, u32[]{:S(2)}) collective-permute-start(bf16[512,512]{1,0:T(8,128)(2,1)S(1)} %bitcast.399), channel_id=1, source_target_pairs={{0,16},{16,0},{1,17},{17,1},{2,18},{18,2},{3,19},{19,3},{4,20},{20... | collective-permute-start | bytes 1572872 | tf_op jit(solution)/shard_map/ppermute | solution.py:237
  81.8 77.5 %collective-permute-start.4 = (bf16[512,2048]{1,0:T(8,128)(2,1)}, bf16[512,2048]{1,0:T(8,128)(2,1)}, u32[]{:S(2)}, u32[]{:S(2)}) collective-permute-start(bf16[512,2048]{1,0:T(8,128)(2,1)} %bitcast.398), channel_id=1, source_target_pairs={{0,16},{16,0},{1,17},{17,1},{2,18},{18,2},{3,19},{19,3},{4,20},{20... | collective-permute-start | bytes 6291464 | tf_op jit(solution)/shard_map/ppermute | solution.py:237
  119.0 41.1 %collective-permute-start.5 = (bf16[2048,512]{1,0:T(8,128)(2,1)}, bf16[2048,512]{1,0:T(8,128)(2,1)}, u32[]{:S(2)}, u32[]{:S(2)}) collective-permute-start(bf16[2048,512]{1,0:T(8,128)(2,1)} %bitcast.480), channel_id=1, source_target_pairs={{0,16},{16,0},{1,17},{17,1},{2,18},{18,2},{3,19},{19,3},{4,20},{20... | collective-permute-start | bytes 6291464 | tf_op jit(solution)/shard_map/ppermute | solution.py:237
  166.4 29.9 %all-to-all-start.2 = ((bf16[256,3,512]{0,1,2:T(4,128)(2,1)}), bf16[256,3,512]{0,1,2:T(4,128)(2,1)S(1)}, u32[]{:S(2)}, u32[]{:S(2)}) async-start(bf16[256,3,512]{0,1,2:T(4,128)(2,1)} %copy.81), calls=%async_computation.2 | async-start | bytes 2097152 | tf_op jit(solution)/shard_map/all_to_all | solution.py:152
  251.3 107.9 %reduce-scatter.13.cloned.1.call-start = ((), (), s32[]{:S(2)}) async-start(), calls=%async_computation.18 | async-start | bytes 327680 | tf_op jit(solution)/shard_map/reduce_scatter | solution.py:257
  259.2 99.9 %reduce-scatter.15.cloned.1.call-start = ((), (), s32[]{:S(2)}) async-start(), calls=%async_computation.19 | async-start | bytes 1310720 | tf_op jit(solution)/shard_map/reduce_scatter | solution.py:257
  262.9 44.4 %collective-permute-start.12 = (bf16[2048,256]{1,0:T(8,128)(2,1)}, bf16[2048,256]{1,0:T(8,128)(2,1)}, u32[]{:S(2)}, u32[]{:S(2)}) collective-permute-start(bf16[2048,256]{1,0:T(8,128)(2,1)} %select_convert_fusion.2), channel_id=1, source_target_pairs={{0,16},{16,0},{1,17},{17,1},{2,18},{18,2},{3,19},{19,3},{4,20},{20... | collective-permute-start | bytes 3145736 | tf_op jit(solution)/shard_map/ppermute | solution.py:237
  302.3 31.3 %all-to-all-start.5 = ((bf16[1024,3,128]{2,1,0:T(4,128)(2,1)}), bf16[1024,3,128]{2,1,0:T(4,128)(2,1)S(1)}, u32[]{:S(2)}, u32[]{:S(2)}) async-start(bf16[1024,3,128]{2,1,0:T(4,128)(2,1)} %copy.89), calls=%async_computation.5 | async-start | bytes 2097152 | tf_op jit(solution)/shard_map/all_to_all | solution.py:198
  307.2 51.9 %reduce-scatter.17.cloned.1.call-start = ((), (), s32[]{:S(2)}) async-start(), calls=%async_computation.20 | async-start | bytes 1310720 | tf_op jit(solution)/shard_map/reduce_scatter | solution.py:257
  311.3 64.4 %reduce-scatter.11.cloned.1.call-start = ((), (), s32[]{:S(2)}) async-start(), calls=%async_computation.17 | async-start | bytes 983040 | tf_op jit(solution)/shard_map/reduce_scatter | solution.py:257
  344.3 162.5 %reduce-scatter.23.cloned.1.call-start = ((), (), s32[]{:S(2)}) async-start(), calls=%async_computation.23 | async-start | bytes 1310720 | tf_op jit(solution)/shard_map/reduce_scatter | solution.py:257
  350.1 156.8 %all-reduce.8.cloned.1.call-start = ((), (), s32[]{:S(2)}) async-start(), calls=%async_computation.28 | async-start | bytes 1572864 | tf_op jit(solution)/shard_map/psum | solution.py:260
  355.8 35.9 %collective-permute-start.16 = (bf16[512,1024]{1,0:T(8,128)(2,1)}, bf16[512,1024]{1,0:T(8,128)(2,1)S(1)}, u32[]{:S(2)}, u32[]{:S(2)}) collective-permute-start(bf16[512,1024]{1,0:T(8,128)(2,1)} %select_convert_fusion.1), channel_id=1, source_target_pairs={{0,16},{16,0},{1,17},{17,1},{2,18},{18,2},{3,19},{19,3},{4,20},{20... | collective-permute-start | bytes 3145736 | tf_op jit(solution)/shard_map/ppermute | solution.py:237
  381.4 125.4 %reduce-scatter.21.cloned.1.call-start = ((), (), s32[]{:S(2)}) async-start(), calls=%async_computation.22 | async-start | bytes 1310720 | tf_op jit(solution)/shard_map/reduce_scatter | solution.py:257
  430.7 43.7 %all-to-all-start.7 = ((bf16[1024,3,128]{2,1,0:T(4,128)(2,1)}), bf16[1024,3,128]{2,1,0:T(4,128)(2,1)}, u32[]{:S(2)}, u32[]{:S(2)}) async-start(bf16[1024,3,128]{2,1,0:T(4,128)(2,1)} %copy.95), calls=%async_computation.7 | async-start | bytes 2097152 | tf_op jit(solution)/shard_map/all_to_all | solution.py:198
  435.0 95.1 %reduce-scatter.19.cloned.1.call-start = ((), (), s32[]{:S(2)}) async-start(), calls=%async_computation.21 | async-start | bytes 327680 | tf_op jit(solution)/shard_map/reduce_scatter | solution.py:257
  438.6 121.0 %reduce-scatter.9.cloned.1.call-start = ((), (), s32[]{:S(2)}) async-start(), calls=%async_computation.16 | async-start | bytes 983040 | tf_op jit(solution)/shard_map/reduce_scatter | solution.py:257
  484.9 122.0 %all-reduce.6.cloned.1.call-start = ((), (), s32[]{:S(2)}) async-start(), calls=%async_computation.27 | async-start | bytes 1572864 | tf_op jit(solution)/shard_map/psum | solution.py:260
  491.1 82.8 %collective-permute-start.6 = (f32[256,512]{1,0:T(8,128)S(1)}, f32[256,512]{1,0:T(8,128)S(1)}, u32[]{:S(2)}, u32[]{:S(2)}) collective-permute-start(f32[256,512]{1,0:T(8,128)S(1)} %get-tuple-element.496), channel_id=1, source_target_pairs={{0,16},{16,0},{1,17},{17,1},{2,18},{18,2},{3,19},{19,3},{4,20},{20... | collective-permute-start | bytes 1572872 | tf_op jit(solution)/shard_map/ppermute | solution.py:237
  (114 other events, 1220.9 us)
Sparse Core Ops, SparseCore 0:
  9.9 33.6 all-gather.9
  45.4 36.3 all-gather.11
  83.7 35.2 all-gather.13
  259.4 24.6 reduce-scatter.12
  287.6 27.6 reduce-scatter.14
  318.6 27.7 reduce-scatter.16
  349.5 26.1 reduce-scatter.10
  378.8 27.7 reduce-scatter.22
  409.2 61.8 all-reduce.7
  474.4 27.9 reduce-scatter.20
  506.0 24.0 reduce-scatter.18
  533.4 26.1 reduce-scatter.8
  562.2 44.6 all-reduce.5

commit v2 on v1

--- a/solution.py
+++ b/solution.py
@@ -324,9 +324,8 @@
     small_sum = jnp.where(is_first, small_zero, small_one) + swap_cores(
         jnp.where(is_first, small_one, small_zero)
     )
-    small_sum = lax.psum(
-        lax.psum_scatter(small_sum, "dp", scatter_dimension=0, tiled=True), "seq"
-    )[0]
+    small_sum = lax.psum(small_sum, ("dp", "seq"))
+    small_sum = lax.dynamic_index_in_dim(small_sum, lax.axis_index("dp"), 0, keepdims=False)
     final_small = (
         small_sum[:gain_size].reshape(1, 2, width),
         small_sum[gain_size : gain_size + shift_size].reshape(1, 6, width),

time: 631 us -> 663 us (1.051)
  blocking collectives: 49.1 us -> 98.4 us
  waiting for transfers between devices: 288 us -> 274 us
    psum x1, blocking collectives: 11.9 us -> 76.7 us  [shards(): small_sum = lax.psum(small_sum, ('dp', 'seq'))]
    psum x2, waiting for transfers between devices: 31.8 us -> 0.02 us  [half_sum(): return lax.psum(own_rows, 'seq')]
    reduce_scatter x8, waiting for transfers between devices: 69.3 us -> 86.3 us  [half_sum(): lax.psum_scatter(total.astype(jnp.bfloat16), 'dp', scatter_dimension=0, t...]
    unnamed x1 -> x0, blocking collectives: 15.6 us -> none
  transfers between devices with their start and end apart: 41 -> 41, of which waited for: 18 -> 17; matrix products, arithmetic and copies ran while one was open for 25% -> 24% of each run, Pallas kernels for 0% -> 0%
where the time goes in v2:
time: 663 us; the launch traced here: 654 us
  waiting for transfers between devices  274 us (41%)
  matrix products  99.8 us (15%)
  blocking collectives  98.4 us (15%)
  other arithmetic  64.4 us (10%)
  local copies, waits for them, and re-layouts  43.7 us (7%)
  starting transfers between devices  42.4 us (6%)
  between operations  17 us (3%)
  loops' own time  15.1 us (2%)
    reduce_scatter x8, waiting for transfers between devices, half_sum(): lax.psum_scatter(total.astype(jnp.bfloat16), 'dp', scatter_dimension=0, t...  86.3 us
    psum x1, blocking collectives, shards(): small_sum = lax.psum(small_sum, ('dp', 'seq'))  76.7 us
    all_gather x3, waiting for transfers between devices, shards(): lax.all_gather(a[0], 'dp', axis=0, tiled=True)  71.1 us
    all_to_all x2, waiting for transfers between devices, section_backward(): lax.all_to_all(grad_packed_heads, 'seq', split_axis=0, concat_axis=2, til...  57.8 us
    all_to_all x2, waiting for transfers between devices, section_forward(): lax.all_to_all(qkv_tokens.reshape(row_count, 3, model_width), 'seq', spli...  26.4 us
    convert_element_type x8, other arithmetic, half_sum(): total.astype(jnp.bfloat16)  20.9 us
    all_to_all x2, waiting for transfers between devices, section_forward(): lax.all_to_all(attended_heads, 'seq', split_axis=0, concat_axis=1, tiled=...  18.3 us
    dot_general x8, matrix products, dot_last(): lax.dot_general(left, right, (((1,), (1,)), ((), ())), preferred_element_...  18.1 us
  transfers between devices with their start and end apart: 41, of which 17 were waited for; matrix products, arithmetic and copies ran while one was open for 24% of the time, Pallas kernels for 0%

profile of v2, /device:TPU:0, one launch (start us, length us, event | category | flops | bytes accessed | tf_op | source)
XLA Modules:
  0.0 654.4 jit_solution(1189899161448385924)
XLA Ops:
  10.1 9.6 %all-gather.5 = bf16[4,1,1536]{2,1,0:T(2,128)(2,1)S(1)} all-gather(bf16[1,1,1536]{2,1,0:T(2,128)(2,1)S(1)} %reshape.637), channel_id=2, replica_groups=mesh['section'=2,'dp'=4,'seq'=4] {'dp'}, dimensions={0}, use_global_device_ids=true | all-gather | bytes 15360 | tf_op jit(solution)/shard_map/all_gather | solution.py:290
  23.5 20.1 %all-gather.10.cloned.1.call-done = bf16[1,512,1536]{2,1,0:T(8,128)(2,1)} async-done(((bf16[1,128,1536]{2,1,0:T(8,128)(2,1)}), bf16[1,512,1536]{2,1,0:T(8,128)(2,1)}) %all-gather.10.cloned.1.call-update) | async-done | bytes 1572880 | tf_op jit(solution)/shard_map/all_gather | solution.py:293
  51.4 4.6 all-to-all-start
  56.0 12.0 %all-gather.2 = bf16[1,512,512]{2,1,0:T(8,128)(2,1)S(1)} all-gather(bf16[1,128,512]{2,1,0:T(8,128)(2,1)S(1)} %copy-done.60), channel_id=4, replica_groups=mesh['section'=2,'dp'=4,'seq'=4] {'dp'}, dimensions={1}, use_global_device_ids=true | all-gather | bytes 655360 | tf_op jit(solution)/shard_map/all_gather | solution.py:293
  68.0 13.8 %all-gather.12.cloned.1.call-done = bf16[1,512,2048]{2,1,0:T(8,128)(2,1)} async-done(((bf16[1,128,2048]{2,1,0:T(8,128)(2,1)}), bf16[1,512,2048]{2,1,0:T(8,128)(2,1)}) %all-gather.12.cloned.1.call-update) | async-done | bytes 2097168 | tf_op jit(solution)/shard_map/all_gather | solution.py:293
  81.8 37.2 %all-gather.14.cloned.1.call-done = bf16[1,2048,512]{2,1,0:T(8,128)(2,1)} async-done(((bf16[1,512,512]{2,1,0:T(8,128)(2,1)}), bf16[1,2048,512]{2,1,0:T(8,128)(2,1)}) %all-gather.14.cloned.1.call-update) | async-done | bytes 2097168 | tf_op jit(solution)/shard_map/all_gather | solution.py:293
  121.1 16.6 %while.56 = (s32[]{:T(128)}, bf16[2,512,2,64]{1,3,2,0:T(8,128)(2,1)S(1)}, f32[2,2,512]{2,1,0:T(2,128)S(1)}, s32[2]{0:T(128)S(1)}, bf16[1024,2,64]{0,2,1:T(8,128)...) while((s32[]{:T(128)}, ...), condition=%wide.region_5.6_spmd.clone, body=%wide.region_2.5_spmd.clone.sunk | while | flops 281607680 | bytes 15503523 | solution.py:80
  142.9 5.1 all-to-all-start.1
  148.1 9.6 %all-to-all-done.1 = bf16[4,256,128]{1,2,0:T(8,128)(2,1)} async-done(((bf16[4,256,128]{1,2,0:T(8,128)(2,1)}), bf16[4,256,128]{1,2,0:T(8,128)(2,1)}, u32[]{:S(2)}, u32[]{:S(2)}) %all-to-all-start.1) | async-done | bytes 262176 | tf_op jit(solution)/shard_map/all_to_all | solution.py:160
  169.9 26.4 %all-to-all-done.2 = bf16[256,3,512]{0,1,2:T(4,128)(2,1)S(1)} async-done(((bf16[256,3,512]{0,1,2:T(4,128)(2,1)}), bf16[256,3,512]{0,1,2:T(4,128)(2,1)S(1)}, u32[]{:S(2)}, u32[]{:S(2)}) %all-to-all-start.2) | async-done | bytes 786464 | tf_op jit(solution)/shard_map/all_to_all | solution.py:152
  198.4 16.6 %while.57 = (s32[]{:T(128)}, bf16[2,512,2,64]{1,3,2,0:T(8,128)(2,1)S(1)}, f32[2,2,512]{2,1,0:T(2,128)S(1)}, s32[2]{0:T(128)S(1)}, bf16[1024,2,64]{0,2,1:T(8,128)...) while((s32[]{:T(128)}, ...), condition=%wide.region_13.14_spmd.clone, body=%wide.region_10.13_spmd.clone.sunk | while | flops 281607680 | bytes 15503523 | solution.py:80
  219.8 8.7 %all-to-all-done.3 = bf16[4,256,128]{1,2,0:T(8,128)(2,1)S(1)} async-done(((bf16[4,256,128]{1,2,0:T(8,128)(2,1)}), bf16[4,256,128]{1,2,0:T(8,128)(2,1)S(1)}, u32[]{:S(2)}, u32[]{:S(2)}) %all-to-all-start.3) | async-done | bytes 262176 | tf_op jit(solution)/shard_map/all_to_all | solution.py:160
  268.1 29.6 %while.58 = (s32[]{:T(128)}, f32[1024,2,64]{0,2,1:T(8,128)S(1)}, f32[1024,2,64]{0,2,1:T(8,128)}, bf16[2,512,2,64]{1,3,2,0:T(8,128)(2,1)}, s32[2]{0:T(128)S(1)}, ...) while((s32[]{:T(128)}, f32[1024,2,64]{0,2,1:T(8,128)S(1)}, ...), condition=%wide.region_20.21_spmd.clone, body=%wide.region_18.20_spmd.clone.sunk | while | flops 688061952 | bytes 76054944 | solution.py:135
  301.7 5.0 all-to-all-start.5
  311.1 22.0 %all-to-all-done.5 = bf16[1024,3,128]{2,1,0:T(4,128)(2,1)S(1)} async-done(((bf16[1024,3,128]{2,1,0:T(4,128)(2,1)}), bf16[1024,3,128]{2,1,0:T(4,128)(2,1)S(1)}, u32[]{:S(2)}, u32[]{:S(2)}) %all-to-all-start.5) | async-done | bytes 786464 | tf_op jit(solution)/shard_map/all_to_all | solution.py:198
  358.7 17.4 %reduce-scatter.11.cloned.1.call-done = bf16[128,768]{1,0:T(8,128)(2,1)} async-done(((bf16[512,768]{1,0:T(8,128)(2,1)}), bf16[128,768]{1,0:T(8,128)(2,1)}) %reduce-scatter.11.cloned.1.call-update) | async-done | bytes 196624 | tf_op jit(solution)/shard_map/reduce_scatter | solution.py:257
  377.3 4.6 all-to-all-start.6
  384.3 7.5 %all-to-all-done.6 = bf16[256,4,128]{2,0,1:T(8,128)(2,1)S(1)} async-done(((bf16[256,4,128]{2,0,1:T(8,128)(2,1)}), bf16[256,4,128]{2,0,1:T(8,128)(2,1)S(1)}, u32[]{:S(2)}, u32[]{:S(2)}) %all-to-all-start.6) | async-done | bytes 262176 | tf_op jit(solution)/shard_map/all_to_all | solution.py:196
  396.9 29.4 %while.59 = (s32[]{:T(128)}, f32[1024,2,64]{0,2,1:T(8,128)S(1)}, f32[1024,2,64]{0,2,1:T(8,128)}, bf16[2,512,2,64]{1,3,2,0:T(8,128)(2,1)}, s32[2]{0:T(128)S(1)}, ...) while((s32[]{:T(128)}, f32[1024,2,64]{0,2,1:T(8,128)S(1)}, ...), condition=%wide.region_27.28_spmd.clone, body=%wide.region_25.27_spmd.clone.sunk | while | flops 688061952 | bytes 76054944 | solution.py:135
  438.3 35.8 %all-to-all-done.7 = bf16[1024,3,128]{2,1,0:T(4,128)(2,1)} async-done(((bf16[1024,3,128]{2,1,0:T(4,128)(2,1)}), bf16[1024,3,128]{2,1,0:T(4,128)(2,1)}, u32[]{:S(2)}, u32[]{:S(2)}) %all-to-all-start.7) | async-done | bytes 786464 | tf_op jit(solution)/shard_map/all_to_all | solution.py:198
  490.8 11.7 %reduce-scatter.21.cloned.1.call-done = bf16[128,1024]{1,0:T(8,128)(2,1)} async-done(((bf16[512,1024]{1,0:T(8,128)(2,1)}), bf16[128,1024]{1,0:T(8,128)(2,1)}) %reduce-scatter.21.cloned.1.call-update) | async-done | bytes 262160 | tf_op jit(solution)/shard_map/reduce_scatter | solution.py:257
  502.5 27.7 %reduce-scatter.19.cloned.1.call-done = bf16[128,256]{1,0:T(8,128)(2,1)} async-done(((bf16[512,256]{1,0:T(8,128)(2,1)}), bf16[128,256]{1,0:T(8,128)(2,1)}) %reduce-scatter.19.cloned.1.call-update) | async-done | bytes 65552 | tf_op jit(solution)/shard_map/reduce_scatter | solution.py:257
  530.2 29.5 %reduce-scatter.9.cloned.1.call-done = bf16[128,768]{1,0:T(8,128)(2,1)} async-done(((bf16[512,768]{1,0:T(8,128)(2,1)}), bf16[128,768]{1,0:T(8,128)(2,1)}) %reduce-scatter.9.cloned.1.call-update) | async-done | bytes 196624 | tf_op jit(solution)/shard_map/reduce_scatter | solution.py:257
  559.7 76.7 %psum.63 = f32[4,1536]{1,0:T(4,128)S(1)} all-reduce(f32[4,1536]{1,0:T(4,128)S(1)} %select_add_fusion), channel_id=1, replica_groups=mesh['section'=2,'dp'=4,'seq'=4] {'dp','seq'}, use_global_device_ids=true, to_apply=%region_48.49 | all-reduce | flops 6144 | bytes 49152 | tf_op jit(solution)/shard_map/psum | solution.py:327
  (511 shorter events, 237.4 us)
Async XLA Ops:
  7.2 36.4 %all-gather.10.cloned.1.call-start = ((), (), s32[]{:S(2)}) async-start(), calls=%async_computation.24 | async-start | bytes 1966080 | tf_op jit(solution)/shard_map/all_gather | solution.py:293
  7.9 73.9 %all-gather.12.cloned.1.call-start = ((), (), s32[]{:S(2)}) async-start(), calls=%async_computation.25 | async-start | bytes 2621440 | tf_op jit(solution)/shard_map/all_gather | solution.py:293
  8.7 110.4 %all-gather.14.cloned.1.call-start = ((), (), s32[]{:S(2)}) async-start(), calls=%async_computation.26 | async-start | bytes 2621440 | tf_op jit(solution)/shard_map/all_gather | solution.py:293
  51.4 67.7 %all-to-all-start = ((bf16[256,3,512]{0,1,2:T(4,128)(2,1)}), bf16[256,3,512]{0,1,2:T(4,128)(2,1)S(1)}, u32[]{:S(2)}, u32[]{:S(2)}) async-start(bf16[256,3,512]{0,1,2:T(4,128)(2,1)} %copy.75), calls=%async_computation | async-start | bytes 2097152 | tf_op jit(solution)/shard_map/all_to_all | solution.py:152
  68.0 80.2 %collective-permute-start.3 = (bf16[512,512]{1,0:T(8,128)(2,1)S(1)}, bf16[512,512]{1,0:T(8,128)(2,1)}, u32[]{:S(2)}, u32[]{:S(2)}) collective-permute-start(bf16[512,512]{1,0:T(8,128)(2,1)S(1)} %bitcast.398), channel_id=1, source_target_pairs={{0,16},{16,0},{1,17},{17,1},{2,18},{18,2},{3,19},{19,3},{4,20},{20... | collective-permute-start | bytes 1572872 | tf_op jit(solution)/shard_map/ppermute | solution.py:237
  81.8 77.5 %collective-permute-start.4 = (bf16[512,2048]{1,0:T(8,128)(2,1)}, bf16[512,2048]{1,0:T(8,128)(2,1)}, u32[]{:S(2)}, u32[]{:S(2)}) collective-permute-start(bf16[512,2048]{1,0:T(8,128)(2,1)} %bitcast.397), channel_id=1, source_target_pairs={{0,16},{16,0},{1,17},{17,1},{2,18},{18,2},{3,19},{19,3},{4,20},{20... | collective-permute-start | bytes 6291464 | tf_op jit(solution)/shard_map/ppermute | solution.py:237
  119.0 41.1 %collective-permute-start.5 = (bf16[2048,512]{1,0:T(8,128)(2,1)}, bf16[2048,512]{1,0:T(8,128)(2,1)}, u32[]{:S(2)}, u32[]{:S(2)}) collective-permute-start(bf16[2048,512]{1,0:T(8,128)(2,1)} %bitcast.479), channel_id=1, source_target_pairs={{0,16},{16,0},{1,17},{17,1},{2,18},{18,2},{3,19},{19,3},{4,20},{20... | collective-permute-start | bytes 6291464 | tf_op jit(solution)/shard_map/ppermute | solution.py:237
  166.4 29.9 %all-to-all-start.2 = ((bf16[256,3,512]{0,1,2:T(4,128)(2,1)}), bf16[256,3,512]{0,1,2:T(4,128)(2,1)S(1)}, u32[]{:S(2)}, u32[]{:S(2)}) async-start(bf16[256,3,512]{0,1,2:T(4,128)(2,1)} %copy.81), calls=%async_computation.2 | async-start | bytes 2097152 | tf_op jit(solution)/shard_map/all_to_all | solution.py:152
  251.2 107.5 %reduce-scatter.13.cloned.1.call-start = ((), (), s32[]{:S(2)}) async-start(), calls=%async_computation.18 | async-start | bytes 327680 | tf_op jit(solution)/shard_map/reduce_scatter | solution.py:257
  259.1 99.6 %reduce-scatter.15.cloned.1.call-start = ((), (), s32[]{:S(2)}) async-start(), calls=%async_computation.19 | async-start | bytes 1310720 | tf_op jit(solution)/shard_map/reduce_scatter | solution.py:257
  262.8 44.0 %collective-permute-start.12 = (bf16[2048,256]{1,0:T(8,128)(2,1)}, bf16[2048,256]{1,0:T(8,128)(2,1)}, u32[]{:S(2)}, u32[]{:S(2)}) collective-permute-start(bf16[2048,256]{1,0:T(8,128)(2,1)} %select_convert_fusion.2), channel_id=1, source_target_pairs={{0,16},{16,0},{1,17},{17,1},{2,18},{18,2},{3,19},{19,3},{4,20},{20... | collective-permute-start | bytes 3145736 | tf_op jit(solution)/shard_map/ppermute | solution.py:237
  301.7 31.4 %all-to-all-start.5 = ((bf16[1024,3,128]{2,1,0:T(4,128)(2,1)}), bf16[1024,3,128]{2,1,0:T(4,128)(2,1)S(1)}, u32[]{:S(2)}, u32[]{:S(2)}) async-start(bf16[1024,3,128]{2,1,0:T(4,128)(2,1)} %copy.89), calls=%async_computation.5 | async-start | bytes 2097152 | tf_op jit(solution)/shard_map/all_to_all | solution.py:198
  306.8 52.0 %reduce-scatter.17.cloned.1.call-start = ((), (), s32[]{:S(2)}) async-start(), calls=%async_computation.20 | async-start | bytes 1310720 | tf_op jit(solution)/shard_map/reduce_scatter | solution.py:257
  310.7 65.5 %reduce-scatter.11.cloned.1.call-start = ((), (), s32[]{:S(2)}) async-start(), calls=%async_computation.17 | async-start | bytes 983040 | tf_op jit(solution)/shard_map/reduce_scatter | solution.py:257
  343.9 146.9 %reduce-scatter.23.cloned.1.call-start = ((), (), s32[]{:S(2)}) async-start(), calls=%async_computation.23 | async-start | bytes 1310720 | tf_op jit(solution)/shard_map/reduce_scatter | solution.py:257
  349.6 141.2 %all-reduce.7.cloned.1.call-start = ((), (), s32[]{:S(2)}) async-start(), calls=%async_computation.28 | async-start | bytes 1572864 | tf_op jit(solution)/shard_map/psum | solution.py:260
  355.4 36.8 %collective-permute-start.16 = (bf16[512,1024]{1,0:T(8,128)(2,1)}, bf16[512,1024]{1,0:T(8,128)(2,1)S(1)}, u32[]{:S(2)}, u32[]{:S(2)}) collective-permute-start(bf16[512,1024]{1,0:T(8,128)(2,1)} %select_convert_fusion.1), channel_id=1, source_target_pairs={{0,16},{16,0},{1,17},{17,1},{2,18},{18,2},{3,19},{19,3},{4,20},{20... | collective-permute-start | bytes 3145736 | tf_op jit(solution)/shard_map/ppermute | solution.py:237
  381.9 120.6 %reduce-scatter.21.cloned.1.call-start = ((), (), s32[]{:S(2)}) async-start(), calls=%async_computation.22 | async-start | bytes 1310720 | tf_op jit(solution)/shard_map/reduce_scatter | solution.py:257
  430.4 43.7 %all-to-all-start.7 = ((bf16[1024,3,128]{2,1,0:T(4,128)(2,1)}), bf16[1024,3,128]{2,1,0:T(4,128)(2,1)}, u32[]{:S(2)}, u32[]{:S(2)}) async-start(bf16[1024,3,128]{2,1,0:T(4,128)(2,1)} %copy.95), calls=%async_computation.7 | async-start | bytes 2097152 | tf_op jit(solution)/shard_map/all_to_all | solution.py:198
  434.7 95.5 %reduce-scatter.19.cloned.1.call-start = ((), (), s32[]{:S(2)}) async-start(), calls=%async_computation.21 | async-start | bytes 327680 | tf_op jit(solution)/shard_map/reduce_scatter | solution.py:257
  438.3 121.3 %reduce-scatter.9.cloned.1.call-start = ((), (), s32[]{:S(2)}) async-start(), calls=%async_computation.16 | async-start | bytes 983040 | tf_op jit(solution)/shard_map/reduce_scatter | solution.py:257
  484.9 154.6 %all-reduce.5.cloned.1.call-start = ((), (), s32[]{:S(2)}) async-start(), calls=%async_computation.27 | async-start | bytes 1572864 | tf_op jit(solution)/shard_map/psum | solution.py:260
  485.2 74.5 %collective-permute-start.7 = (f32[4,1536]{1,0:T(4,128)S(1)}, f32[4,1536]{1,0:T(4,128)S(1)}, u32[]{:S(2)}, u32[]{:S(2)}) collective-permute-start(f32[4,1536]{1,0:T(4,128)S(1)} %broadcast_select_fusion.39), channel_id=1, source_target_pairs={{0,16},{16,0},{1,17},{17,1},{2,18},{18,2},{3,19},{19,3},{4,20},{20... | collective-permute-start | bytes 73736 | tf_op jit(solution)/shard_map/ppermute | solution.py:237
  490.7 147.6 %collective-permute-start.6 = (f32[256,512]{1,0:T(8,128)S(1)}, f32[256,512]{1,0:T(8,128)S(1)}, u32[]{:S(2)}, u32[]{:S(2)}) collective-permute-start(f32[256,512]{1,0:T(8,128)S(1)} %get-tuple-element.496), channel_id=1, source_target_pairs={{0,16},{16,0},{1,17},{17,1},{2,18},{18,2},{3,19},{19,3},{4,20},{20... | collective-permute-start | bytes 1572872 | tf_op jit(solution)/shard_map/ppermute | solution.py:237
  (113 other events, 1084.8 us)
Sparse Core Ops, SparseCore 0:
  9.9 33.6 all-gather.9
  45.4 36.3 all-gather.11
  83.7 35.2 all-gather.13
  259.3 25.1 reduce-scatter.12
  288.1 27.7 reduce-scatter.14
  319.1 27.7 reduce-scatter.16
  350.1 26.0 reduce-scatter.10
  379.3 27.7 reduce-scatter.22
  409.7 61.1 all-reduce.6
  474.2 28.2 reduce-scatter.20
  506.1 24.0 reduce-scatter.18
  533.5 26.0 reduce-scatter.8
  562.2 45.6 all-reduce.4
